TPU v7x, 128 devices: a whole 4x4x4 slice. The times are simulated.
128 devices in a mesh: dom: 4 (over x), sub: 32 (over z, y, core).
Axes of the slice: x: 4, y: 4, z: 4, core: 2. Of those that a mesh axis runs over, the one named last changes fastest.
Arguments:
- history: float32 [4, 192, 32768], P(None, None, ('dom', 'sub')), may hold values from -1.5 to 1.5
- diag_blocks: bfloat16 [1152, 32768], P(None, ('dom', 'sub')), may hold values from -1.25 to 1.25
- pair_blocks: bfloat16 [1152, 393216], P(None, ('dom', 'sub')), may hold values from -0.25 to 0.25
- neighbours: int32 [393216], P(('dom', 'sub')), may hold values from 0 to 32767, as said below
- counts: int32 [128], P(('dom', 'sub')), may hold values from 64 to 256, as said below
Outputs:
- products: float32 [384, 32768], P(None, ('dom', 'sub'))
- pair_scores: float32 [128, 393216], P(None, ('dom', 'sub'))
Inputs may be any that keep to these rules, and one draw needn't show every extreme that they name: `neighbours`: entry p of the device block of 3072 entries belongs to that device's molecule slot p // 12. Every entry names a live molecule of a device whose dom index differs from the entry's own device's by at most one, periodically, with any sub index. Of one device's block, at most 64 entries name molecules of any one device, and some device is named exactly 64 times. `counts`: the live molecules of a device are its first count slots; some device holds 256.
All inputs are finite; a program needn't handle non-finite values.
Results may differ from a plain program's by a relative error of at most 0.006.
Values may be sent and summed in bfloat16 or wider, within the bound.
No kernel may reach another device: no remote copies, remote signals or barrier semaphores. Data moves between devices by JAX's collectives and lax.ppermute only.
A program may use at most 256 MiB of HBM per device.

v0:
```python
import jax
import jax.numpy as jnp
from jax import lax
from jax.sharding import PartitionSpec as P

BAS = 24
OCC = 8


ASPC_WEIGHTS = (2.8, -2.8, 1.2, -0.2)


def with_halo(block, sides, width):
    for axis, dim in sides:
        count = lax.axis_size(axis)
        forward = [(i, i + 1) for i in range(count - 1)]
        forward.append((count - 1, 0))
        backward = [(target, source) for source, target in forward]
        low = lax.ppermute(
            lax.slice_in_dim(block, block.shape[dim] - width, None, axis=dim), axis, forward
        )
        high = lax.ppermute(lax.slice_in_dim(block, 0, width, axis=dim), axis, backward)
        block = jnp.concatenate([low, block, high], axis=dim)
    return block


def shifted(block, axis, distance):
    devices = range(lax.axis_size(axis))
    route = [((i - distance) % len(devices), i) for i in devices]
    return lax.ppermute(block, axis, route)


def predict(history):
    total = ASPC_WEIGHTS[0] * history[0]
    for level in range(1, 4):
        total = total + ASPC_WEIGHTS[level] * history[level]
    return total.astype(jnp.bfloat16)


def expander(molecules, per_mol, dtype):
    column = jnp.arange(molecules * per_mol, dtype=jnp.int32) // per_mol
    return (jnp.arange(molecules, dtype=jnp.int32)[:, None] == column[None, :]).astype(dtype)


def spread_rows(values, per_mol):
    table = expander(values.shape[1], per_mol, jnp.bfloat16)
    return jnp.dot(values, table, preferred_element_type=jnp.float32).astype(jnp.bfloat16)


def collapse_rows(values, per_mol):
    molecules = values.shape[1] // per_mol
    table = expander(molecules, per_mol, jnp.float32)
    return lax.dot_general(
        values,
        table,
        (((1,), (1,)), ((), ())),
        precision=lax.Precision.HIGHEST,
        preferred_element_type=jnp.float32,
    )


def pair_terms(blocks, mine, theirs):
    width = blocks.shape[1]
    square = blocks.reshape(2, BAS, BAS, width)
    own = mine.reshape(BAS, OCC, width).astype(jnp.float32)
    other = theirs.reshape(BAS, OCC, width).astype(jnp.float32)
    applied = jnp.zeros((2, BAS, OCC, width), jnp.float32)
    for inner in range(BAS):
        applied = (
            applied + square[:, :, inner, None, :].astype(jnp.float32) * other[None, None, inner]
        )
    reduced = jnp.zeros((2, OCC, OCC, width), jnp.float32)
    turned = jnp.zeros((2, BAS, OCC, width), jnp.float32)
    for inner in range(BAS):
        reduced = reduced + own[inner][None, :, None, :] * applied[:, inner][:, None, :, :]
        turned = turned + square[:, inner, :, None, :].astype(jnp.float32) * own[inner][None, None]
    return (
        applied.reshape(2 * BAS * OCC, width),
        reduced.reshape(2 * OCC * OCC, width),
        turned.reshape(2 * BAS * OCC, width),
    )


def on_device(history, diag_blocks, pair_blocks, neighbours, counts):
    mols = history.shape[2]
    pairs = pair_blocks.shape[1]
    per_mol = pairs // mols
    rows = 2 * BAS * OCC
    teams = lax.axis_size("sub")
    domains = lax.axis_size("dom")
    my_domain = lax.axis_index("dom")
    count = counts[0]
    guess = predict(history)
    owner = neighbours // mols
    slot = neighbours % mols
    offset = (owner // teams - my_domain + 1) % domains
    team = owner % teams
    target = offset * (teams * mols) + team * mols + slot
    team_all = lax.all_gather(guess, "sub", axis=1, tiled=True)
    near = with_halo(team_all, (("dom", 1),), teams * mols)
    mine = spread_rows(guess, per_mol)
    theirs = jnp.take(near, target, axis=1)
    live = (jnp.arange(pairs) // per_mol < count).astype(jnp.float32)
    applied, reduced, turned = pair_terms(pair_blocks, mine, theirs)
    forward = collapse_rows(applied * live, per_mol)
    scores = reduced * live
    sent = turned * live
    back = jnp.zeros((rows, 3 * teams * mols), jnp.float32).at[:, target].add(sent)
    back = back.reshape(rows, 3, teams * mols)
    summed = lax.psum_scatter(back, "sub", scatter_dimension=2, tiled=True)
    from_lower = shifted(summed[:, 2], "dom", 1)
    from_upper = shifted(summed[:, 0], "dom", -1)
    returned = summed[:, 1] + from_lower + from_upper
    square = diag_blocks.reshape(2, BAS, BAS, mols)
    own = guess.reshape(BAS, OCC, mols).astype(jnp.float32)
    local = jnp.zeros((2, BAS, OCC, mols), jnp.float32)
    for inner in range(BAS):
        local = local + square[:, :, inner, None, :].astype(jnp.float32) * own[None, None, inner]
    local = local.reshape(rows, mols)
    alive = (jnp.arange(mols) < count).astype(jnp.float32)
    return ((local + forward + returned) * alive, scores)


def solution(mesh):
    in_specs = (
        P(None, None, ("dom", "sub")),
        P(None, ("dom", "sub")),
        P(None, ("dom", "sub")),
        P(("dom", "sub")),
        P(("dom", "sub")),
    )
    out_specs = (P(None, ("dom", "sub")), P(None, ("dom", "sub")))
    return jax.shard_map(
        on_device, mesh=mesh, in_specs=in_specs, out_specs=out_specs, check_vma=False
    )
```

profile of v0, /device:TPU:6, one launch (start us, length us, event | category | flops | bytes accessed | tf_op | source)
XLA Modules:
  0.0 559.9 jit_solution(593381488718602885)
XLA Ops:
  9.9 25.0 %fusion.77 = (bf16[2,24,1,3072]{3,2,1,0:T(2,128)(2,1)}, bf16[2,24,1,3072]{3,2,1,0:T(2,128)(2,1)S(1)}, bf16[2,24,1,3072]{3,2,1,0:T(2,128)(2,1)S(1)}, bf16[2,24,1,...) fusion(bf16[2,24,24,3072]{3,2,1,0:T(8,128)(2,1)} %bitcast.646), kind=kLoop, calls=%fused_computation.348 | loop fusion | bytes 11206656 | tf_op jit(solution)/shard_map/slice | solution.py:70
  35.0 8.6 %fusion.78 = (bf16[2,24,1,3072]{3,2,1,0:T(2,128)(2,1)}, bf16[2,24,1,3072]{3,2,1,0:T(2,128)(2,1)}, bf16[2,24,1,3072]{3,2,1,0:T(2,128)(2,1)}, bf16[2,24,1,3072]{3,2,1,0:T(2,128)(2,1)}, bf16[2,24,1,3072]{3,2,1,0:T(2,128)(2,1)}) fusion(bf16[2,24,24,3072]{3,2,1,0:T(8,128)(2,1)} %bitcast.647), kind=kLoop, calls=%fused_computation.349 | loop fusion | bytes 2949120 | tf_op jit(solution)/shard_map/slice | solution.py:70
  73.4 4.7 broadcast_multiply_fusion.4
  78.1 4.7 broadcast_multiply_fusion.6
  82.8 5.9 %copy.239 = bf16[192,8192]{1,0:T(8,128)(2,1)} copy(bf16[192,8192]{0,1:T(8,128)(2,1)} %bitcast.657) | data formatting | bytes 6291456 | tf_op jit(solution)/shard_map/all_gather | solution.py:99
  90.8 6.3 %broadcast_multiply_fusion.2 = (f32[2,24,8,3072]{3,2,1,0:T(8,128)}, f32[2,24,8,3072]{3,2,1,0:T(8,128)}) fusion(f32[8,3072]{1,0:T(8,128)} %get-tuple-element.83, f32[2,24,3072]{2,1,0:T(8,128)} %get-tuple-element.9, f32[8,3072]{1,0:T(8,128)} %get-tuple-element.84, f32[2,24,3072]{2,1,0:T(8,128)} %get-tuple-element.10), kind=kLoop, calls=%fused_computation.32 | loop fusion | flops 2359296 | bytes 10813440 | tf_op jit(solution)/shard_map/mul | solution.py:76
  97.5 5.8 %broadcast_multiply_fusion = (f32[2,24,8,3072]{3,2,1,0:T(8,128)}, f32[2,24,8,3072]{3,2,1,0:T(8,128)}) fusion(f32[8,3072]{1,0:T(8,128)S(1)} %copy-done.88, f32[2,24,3072]{2,1,0:T(8,128)S(1)} %copy-done.53, f32[8,3072]{1,0:T(8,128)S(1)} %copy-done.90, f32[2,24,3072]{2,1,0:T(8,128)S(1)} %copy-done.54), kind=kLoop, calls=%fused_computation.30 | loop fusion | flops 2359296 | bytes 10813440 | tf_op jit(solution)/shard_map/mul | solution.py:76
  104.6 7.3 %add_add_fusion = f32[2,24,8,3072]{3,2,1,0:T(8,128)} fusion(f32[8,3072]{1,0:T(8,128)S(1)} %copy-done.68, f32[2,24,3072]{2,1,0:T(8,128)S(1)} %copy-done.7, f32[8,3072]{1,0:T(8,128)S(1)} %copy-done.70, f32[2,24,3072]{2,1,0:T(8,128)S(1)} %copy-done.8, f32[8,3072]{1,0:T(8,128)S(1)} %copy-done.72, f32[2,24,3072]{2,1,0:T(8,128)S(1)} %copy-done.9, ...), kind=kLoop, calls=%fused_computation.23 | loop fusion | flops 36569088 | bytes 15728640 | tf_op jit(solution)/shard_map/add | solution.py:76
  111.8 47.1 %collective-permute-done = bf16[192,8192]{1,0:T(8,128)(2,1)} collective-permute-done((bf16[192,8192]{1,0:T(8,128)(2,1)}, bf16[192,8192]{1,0:T(8,128)(2,1)}, u32[]{:S(2)}, u32[]{:S(2)}) %collective-permute-start) | collective-permute-done | bytes 3145760 | tf_op jit(solution)/shard_map/ppermute | solution.py:19
  159.0 5.9 %copy.241 = bf16[192,8192]{0,1:T(8,128)(2,1)} copy(bf16[192,8192]{1,0:T(8,128)(2,1)} %collective-permute-done) | data formatting | bytes 6291456 | tf_op jit(solution)/shard_map/ppermute | solution.py:19
  164.9 5.9 %copy.242 = bf16[192,8192]{0,1:T(8,128)(2,1)} copy(bf16[192,8192]{1,0:T(8,128)(2,1)} %collective-permute-done.1) | data formatting | bytes 6291456 | tf_op jit(solution)/shard_map/ppermute | solution.py:22
  170.8 16.3 %pad_maximum_fusion = bf16[192,24576]{0,1:T(8,128)(2,1)} fusion(bf16[192,8192]{0,1:T(8,128)(2,1)} %copy.242, bf16[192,8192]{0,1:T(8,128)(2,1)} %bitcast.658, bf16[192,8192]{0,1:T(8,128)(2,1)} %copy.241), kind=kLoop, calls=%fused_computation.4 | loop fusion | flops 28311552 | bytes 18874368 | tf_op jit(solution)/shard_map/concatenate | solution.py:23
  187.1 19.4 %gather_fusion = bf16[3072,192]{1,0:T(8,128)(2,1)} fusion(bf16[192,24576]{0,1:T(8,128)(2,1)} %pad_maximum_fusion, s32[3072]{0:T(1024)} %broadcast_clamp_fusion), kind=kCustom, calls=%fused_computation | custom fusion | bytes 2371584 | tf_op jit(solution)/shard_map/jit(_take)/gather | solution.py:102
  210.7 4.9 broadcast_multiply_fusion.10
  215.5 4.7 broadcast_multiply_fusion.12
  220.3 4.7 broadcast_multiply_fusion.14
  225.1 5.8 %broadcast_multiply_fusion.8 = (f32[2,24,8,3072]{3,2,1,0:T(8,128)}, f32[2,24,8,3072]{3,2,1,0:T(8,128)}) fusion(f32[8,3072]{1,0:T(8,128)S(1)} %get-tuple-element.105, f32[2,24,3072]{2,1,0:T(8,128)S(1)} %fusion.39, f32[8,3072]{1,0:T(8,128)S(1)} %get-tuple-element.106, f32[2,24,3072]{2,1,0:T(8,128)S(1)} %fusion.40), kind=kLoop, calls=%fused_computation.38 | loop fusion | flops 2359296 | bytes 10813440 | tf_op jit(solution)/shard_map/mul | solution.py:70
  232.0 10.8 %add_add_fusion.2 = (f32[2,24,8,3072]{3,2,1,0:T(8,128)}, f32[2,24,8,3072]{3,2,1,0:T(8,128)}) fusion(f32[8,3072]{1,0:T(8,128)S(1)} %get-tuple-element.112, f32[2,24,3072]{2,1,0:T(8,128)S(1)} %copy-done.2, f32[8,3072]{1,0:T(8,128)S(1)} %get-tuple-element.111, f32[2,24,3072]{2,1,0:T(8,128)S(1)} %copy-done.1, f32[8,3072]{1,0:T(8,128)S(1)} %get-tuple-element.110, ...), kind=kLoop, calls=%fused_computation.25 | loop fusion | flops 55443456 | bytes 25952256 | tf_op jit(solution)/shard_map/add | solution.py:70
  242.8 33.9 %fusion.2 = (f32[384,3072]{1,0:T(8,128)}, f32[384,3072]{1,0:T(8,128)}) fusion(f32[2,24,8,3072]{3,2,1,0:T(8,128)} %get-tuple-element.184, f32[2,24,8,3072]{3,2,1,0:T(8,128)} %get-tuple-element.185, f32[2,24,8,3072]{3,2,1,0:T(8,128)} %get-tuple-element.186, f32[2,24,8,3072]{3,2,1,0:T(8,128)} %get-tuple-element.187, f32[2,24,8,3072]{3,2,1,0:T(8,128)} %get-tuple-element.188, ...), kind=kLoop, calls=%fused_computation.6 | loop fusion | flops 21233664 | bytes 94384128 | tf_op jit(solution)/shard_map/mul | solution.py:107
  276.6 6.0 %copy.291 = f32[3072,384]{1,0:T(8,128)} copy(f32[3072,384]{0,1:T(8,128)} %bitcast.654) | data formatting | bytes 9437184 | tf_op jit(solution)/shard_map/mul | solution.py:107
  282.7 34.1 %scatter_custom_fusion = f32[384,24576]{0,1:T(8,128)} fusion(s32[3072]{0:T(1024)} %copy-done.104, f32[3072,384]{1,0:T(8,128)} %copy.291, f32[]{:T(128)} %constant.105.clone.1), kind=kCustom, calls=%fused_computation.2 | custom fusion | flops 1179648 | bytes 37749248 | tf_op jit(solution)/shard_map/scatter-add | solution.py:108
  316.8 36.9 %copy.292 = f32[384,3,8192]{2,0,1:T(8,128)} copy(f32[384,3,8192]{0,2,1:T(8,128)} %bitcast.645) | data formatting | bytes 75497472 | tf_op jit(solution)/shard_map/reshape | solution.py:109
  372.6 162.3 %reduce-scatter.2.cloned.1.call-done = f32[384,3,256]{2,0,1:T(8,128)} async-done(((f32[384,3,8192]{2,0,1:T(8,128)}), f32[384,3,256]{2,0,1:T(8,128)}) %reduce-scatter.2.cloned.1.call-update) | async-done | bytes 1179664 | tf_op jit(solution)/shard_map/reduce_scatter | solution.py:110
  538.2 7.3 %fusion.6 = f32[128,3072]{1,0:T(8,128)} fusion(f32[2,8,8,3072]{3,2,1,0:T(8,128)} %get-tuple-element.192, f32[2,8,8,3072]{3,2,1,0:T(8,128)} %get-tuple-element.193, f32[2,8,8,3072]{3,2,1,0:T(8,128)} %get-tuple-element.194, f32[2,8,8,3072]{3,2,1,0:T(8,128)} %get-tuple-element.195, f32[2,8,8,3072]{3,2,1,0:T(8,128)} %get-tuple-element.196, ...), kind=kLoop, calls=%fused_computation.47 | loop fusion | flops 3538944 | bytes 15740928 | tf_op jit(solution)/shard_map/mul | solution.py:106
  (342 shorter events, 68.9 us)
Async XLA Ops:
  7.2 75.7 %all-gather.3.cloned.1.call-start = ((), (), s32[]{:S(2)}) async-start(), calls=%async_computation.2 | async-start | bytes 4325376 | tf_op jit(solution)/shard_map/all_gather | solution.py:99
  9.9 525.1 %reduce-scatter.2.cloned.1.call-start = ((), (), s32[]{:S(2)}) async-start(), calls=%async_computation.1 | async-start | bytes 38928384 | tf_op jit(solution)/shard_map/reduce_scatter | solution.py:110
  43.6 18.6 %copy-start.102 = (s32[3072]{0:T(1024)}, s32[3072]{0:T(1024)S(1)}, u32[]{:S(2)}) copy-start(s32[3072]{0:T(1024)S(1)} %add_select_fusion) | copy-start | bytes 36868
  44.0 7.7 %copy-start.47 = (bf16[2,24,1,3072]{3,2,1,0:T(2,128)(2,1)S(1)}, bf16[2,24,1,3072]{3,2,1,0:T(2,128)(2,1)}, u32[]{:S(2)}) copy-start(bf16[2,24,1,3072]{3,2,1,0:T(2,128)(2,1)} %get-tuple-element.44) | copy-start | bytes 884740
  44.2 8.6 %copy-start.46 = (bf16[2,24,1,3072]{3,2,1,0:T(2,128)(2,1)S(1)}, bf16[2,24,1,3072]{3,2,1,0:T(2,128)(2,1)}, u32[]{:S(2)}) copy-start(bf16[2,24,1,3072]{3,2,1,0:T(2,128)(2,1)} %get-tuple-element.45) | copy-start | bytes 884740
  44.7 8.9 %copy-start.45 = (bf16[2,24,1,3072]{3,2,1,0:T(2,128)(2,1)S(1)}, bf16[2,24,1,3072]{3,2,1,0:T(2,128)(2,1)}, u32[]{:S(2)}) copy-start(bf16[2,24,1,3072]{3,2,1,0:T(2,128)(2,1)} %get-tuple-element.46) | copy-start | bytes 884740
  44.8 9.8 %copy-start.44 = (bf16[2,24,1,3072]{3,2,1,0:T(2,128)(2,1)S(1)}, bf16[2,24,1,3072]{3,2,1,0:T(2,128)(2,1)}, u32[]{:S(2)}) copy-start(bf16[2,24,1,3072]{3,2,1,0:T(2,128)(2,1)} %get-tuple-element.47) | copy-start | bytes 884740
  46.9 8.8 %copy-start.43 = (bf16[2,24,1,3072]{3,2,1,0:T(2,128)(2,1)S(1)}, bf16[2,24,1,3072]{3,2,1,0:T(2,128)(2,1)}, u32[]{:S(2)}) copy-start(bf16[2,24,1,3072]{3,2,1,0:T(2,128)(2,1)} %get-tuple-element.48) | copy-start | bytes 884740
  51.8 7.6 %copy-start.39 = (bf16[2,24,1,3072]{3,2,1,0:T(2,128)(2,1)S(1)}, bf16[2,24,1,3072]{3,2,1,0:T(2,128)(2,1)}, u32[]{:S(2)}) copy-start(bf16[2,24,1,3072]{3,2,1,0:T(2,128)(2,1)} %get-tuple-element.52) | copy-start | bytes 884740
  53.7 7.6 %copy-start.37 = (bf16[2,24,1,3072]{3,2,1,0:T(2,128)(2,1)S(1)}, bf16[2,24,1,3072]{3,2,1,0:T(2,128)(2,1)}, u32[]{:S(2)}) copy-start(bf16[2,24,1,3072]{3,2,1,0:T(2,128)(2,1)} %get-tuple-element.54) | copy-start | bytes 884740
  57.5 7.7 %copy-start.36 = (bf16[2,24,1,3072]{3,2,1,0:T(2,128)(2,1)S(1)}, bf16[2,24,1,3072]{3,2,1,0:T(2,128)(2,1)}, u32[]{:S(2)}) copy-start(bf16[2,24,1,3072]{3,2,1,0:T(2,128)(2,1)} %get-tuple-element.55) | copy-start | bytes 884740
  58.5 7.6 %copy-start.35 = (bf16[2,24,1,3072]{3,2,1,0:T(2,128)(2,1)S(1)}, bf16[2,24,1,3072]{3,2,1,0:T(2,128)(2,1)}, u32[]{:S(2)}) copy-start(bf16[2,24,1,3072]{3,2,1,0:T(2,128)(2,1)} %get-tuple-element.51) | copy-start | bytes 884740
  58.5 9.7 %slice-start = ((s8[7077888]{0:T(1024)(128)(4,1)}), s8[4194304]{0:T(1024)(128)(4,1)S(1)}, s32[]{:S(2)}) async-start(s8[7077888]{0:T(1024)(128)(4,1)} %bitcast.648), calls=%async_computation.3 | async-start | bytes 8388608
  68.2 9.9 %copy-start.98 = (f32[8,3072]{1,0:T(8,128)}, f32[8,3072]{1,0:T(8,128)S(1)}, u32[]{:S(2)}) copy-start(f32[8,3072]{1,0:T(8,128)S(1)} %get-tuple-element.87) | copy-start | bytes 294916
  68.2 9.9 %copy-start.100 = (f32[8,3072]{1,0:T(8,128)}, f32[8,3072]{1,0:T(8,128)S(1)}, u32[]{:S(2)}) copy-start(f32[8,3072]{1,0:T(8,128)S(1)} %get-tuple-element.88) | copy-start | bytes 294916
  88.7 70.2 %collective-permute-start = (bf16[192,8192]{1,0:T(8,128)(2,1)}, bf16[192,8192]{1,0:T(8,128)(2,1)}, u32[]{:S(2)}, u32[]{:S(2)}) collective-permute-start(bf16[192,8192]{1,0:T(8,128)(2,1)} %copy.239), channel_id=1, source_target_pairs={{0,32},{32,64},{64,96},{96,0},{1,33},{33,65},{65,97},{97,1},{2,34}... | collective-permute-start | bytes 9437192 | tf_op jit(solution)/shard_map/ppermute | solution.py:19
  89.1 75.7 %collective-permute-start.1 = (bf16[192,8192]{1,0:T(8,128)(2,1)}, bf16[192,8192]{1,0:T(8,128)(2,1)}, u32[]{:S(2)}, u32[]{:S(2)}) collective-permute-start(bf16[192,8192]{1,0:T(8,128)(2,1)} %copy.239), channel_id=1, source_target_pairs={{32,0},{64,32},{96,64},{0,96},{33,1},{65,33},{97,65},{1,97},{34,2}... | collective-permute-start | bytes 9437192 | tf_op jit(solution)/shard_map/ppermute | solution.py:22
  90.8 12.5 %copy-start.84 = (f32[8,3072]{1,0:T(8,128)S(1)}, f32[8,3072]{1,0:T(8,128)}, u32[]{:S(2)}) copy-start(f32[8,3072]{1,0:T(8,128)} %get-tuple-element.97) | copy-start | bytes 294916
  90.8 12.5 %copy-start.86 = (f32[8,3072]{1,0:T(8,128)S(1)}, f32[8,3072]{1,0:T(8,128)}, u32[]{:S(2)}) copy-start(f32[8,3072]{1,0:T(8,128)} %get-tuple-element.98) | copy-start | bytes 294916
  369.7 178.7 %slice-start.2 = ((s8[4718592]{0:T(1024)(128)(4,1)}), s8[524288]{0:T(1024)(128)(4,1)S(1)}, s32[]{:S(2)}) async-start(s8[4718592]{0:T(1024)(128)(4,1)} %bitcast.652), calls=%async_computation.5 | async-start | bytes 1048576
  536.1 10.8 %collective-permute-start.2 = (f32[384,256]{1,0:T(8,128)S(1)}, f32[384,256]{1,0:T(8,128)S(1)}, u32[]{:S(2)}, u32[]{:S(2)}) collective-permute-start(f32[384,256]{1,0:T(8,128)S(1)} %get-tuple-element.128), channel_id=1, source_target_pairs={{96,0},{0,32},{32,64},{64,96},{97,1},{1,33},{33,65},{65,97},{98,2}... | collective-permute-start | bytes 1179656 | tf_op jit(solution)/shard_map/ppermute | solution.py:30
  536.7 11.7 %collective-permute-start.3 = (f32[384,256]{1,0:T(8,128)S(1)}, f32[384,256]{1,0:T(8,128)S(1)}, u32[]{:S(2)}, u32[]{:S(2)}) collective-permute-start(f32[384,256]{1,0:T(8,128)S(1)} %get-tuple-element.129), channel_id=1, source_target_pairs={{32,0},{64,32},{96,64},{0,96},{33,1},{65,33},{97,65},{1,97},{34,2}... | collective-permute-start | bytes 1179656 | tf_op jit(solution)/shard_map/ppermute | solution.py:30
  538.2 10.2 %slice-start.3 = ((s8[4718592]{0:T(1024)(128)(4,1)}), s8[4194304]{0:T(1024)(128)(4,1)S(1)}, s32[]{:S(2)}) async-start(s8[4718592]{0:T(1024)(128)(4,1)} %bitcast.652), calls=%async_computation.6 | async-start | bytes 8388608
  538.2 10.2 %copy-start.103 = (s32[3072]{0:T(1024)S(1)}, s32[3072]{0:T(1024)}, u32[]{:S(2)}) copy-start(s32[3072]{0:T(1024)} %copy-done.102) | copy-start | bytes 36868
  (94 other events, 552.1 us)
Sparse Core Ops, SparseCore 0:
  10.3 48.7 all-gather.2
  353.9 181.0 reduce-scatter.1
where the time goes:
time: 567 us; the launch traced here: 560 us
  waiting for transfers between devices  212 us (37%)
  other arithmetic  192 us (34%)
  local copies, waits for them, and re-layouts  130 us (23%)
  between operations  16.3 us (3%)
    reduce_scatter x1, waiting for transfers between devices, on_device(): summed = lax.psum_scatter(back, 'sub', scatter_dimension=2, tiled=True)  162 us
    ppermute x1, waiting for transfers between devices, with_halo(): lax.ppermute(lax.slice_in_dim(block, block.shape[dim] - width, None, axis...  47.1 us
    mul x28, other arithmetic, pair_terms(): square[:, :, inner, None, :].astype(jnp.float32) * other[None, None, inner]  40 us
    reshape x1, local copies, waits for them, and re-layouts, on_device(): back = back.reshape(rows, 3, teams * mols)  36.9 us
    scatter-add x1, other arithmetic, on_device(): jnp.zeros((rows, 3 * teams * mols), jnp.float32).at[:, target].add(sent)  34.1 us
    mul x1, other arithmetic, on_device(): sent = turned * live  33.9 us
    slice x2, local copies, waits for them, and re-layouts, pair_terms(): square[:, :, inner, None, :].astype(jnp.float32) * other[None, None, inner]  33.7 us
    gather x2, local copies, waits for them, and re-layouts, on_device(): theirs = jnp.take(near, target, axis=1)  22 us
  transfers between devices with their start and end apart: 6, of which 4 were waited for; matrix products, arithmetic and copies ran while one was open for 21% of the time, Pallas kernels for 0%

commit v1 on v0

v1 whole, which is shorter than its diff:
```python
import functools

import jax
import jax.numpy as jnp
from jax import lax
from jax.experimental import pallas as pl
from jax.experimental.pallas import tpu as pltpu
from jax.sharding import PartitionSpec as P

BAS = 24
OCC = 8
FEAT = BAS * OCC
ROWS = 2 * FEAT
CAP = 64
LANES = 128
SIDES = 3
ASPC_WEIGHTS = (2.8, -2.8, 1.2, -0.2)
VMEM = pl.BlockSpec(memory_space=pltpu.VMEM)
SMEM = pl.BlockSpec(memory_space=pltpu.SMEM)
NT = (((1,), (1,)), ((), ()))


def iota(shape, dim):
    return lax.broadcasted_iota(jnp.int32, shape, dim)


def prepare_kernel(teams, domains, info, history, near, guess, rows, dest, index, label):
    mols = guess.shape[1]
    total = ASPC_WEIGHTS[0] * history[0]
    for level in range(1, 4):
        total = total + ASPC_WEIGHTS[level] * history[level]
    rounded = total.astype(jnp.bfloat16)
    guess[...] = rounded
    wide = rounded.astype(jnp.float32)
    for part in range(mols // LANES):
        cut = slice(part * LANES, (part + 1) * LANES)
        rows[cut, :] = wide[:LANES, cut].T.astype(jnp.bfloat16)
    rest = jnp.concatenate([wide[LANES:, :LANES], wide[LANES:, LANES:]], axis=0)
    rows[mols:, :] = rest.T.astype(jnp.bfloat16)

    my_domain = info[0]
    parity = info[2]
    listed = near[...]
    owner = listed // mols
    slot = listed % mols
    team = owner % teams
    offset = (owner // teams - my_domain + 1 + domains) % domains
    base = (team * SIDES + offset) * rows.shape[0]
    index[0] = base + slot
    index[1] = base + mols + slot % LANES
    index[2] = slot // LANES
    place = team * (SIDES * CAP) + offset * CAP
    key = team * 8 + offset
    keys = teams * 8
    square = (LANES, 2 * LANES)
    before = ((iota(square, 0) < iota(square, 1)) | (iota(square, 1) >= LANES)).astype(jnp.bfloat16)
    which = iota((keys, LANES), 0)
    carry = jnp.zeros((keys, LANES), jnp.float32)
    names = jnp.zeros((keys, LANES), jnp.float32)
    for block in range(listed.shape[0]):
        hit = which == key[block : block + 1]
        ones = jnp.where(hit, 1.0, 0.0)
        sums = jnp.dot(ones.astype(jnp.bfloat16), before, preferred_element_type=jnp.float32)
        prior = sums[:, :LANES] + carry
        carry = carry + sums[:, LANES:]
        rank = jnp.sum(jnp.where(hit, prior, 0.0), axis=0, keepdims=True).astype(jnp.int32)
        dest[block : block + 1, :] = place[block : block + 1] + rank
        column = iota((LANES, LANES), 0) == rank + parity * CAP
        named = jnp.where(hit, slot[block : block + 1].astype(jnp.float32), 0.0)
        names = names + lax.dot_general(
            named.astype(jnp.bfloat16),
            column.astype(jnp.bfloat16),
            NT,
            preferred_element_type=jnp.float32,
        )
    label[...] = names


def spread(guess, first, per_mol, count):
    mols = guess.shape[1]
    mol = iota((mols, LANES), 0)
    pair = iota((mols, LANES), 1) + first
    table = (pair >= mol * per_mol) & (pair < (mol + 1) * per_mol) & (mol < count)
    return jnp.dot(
        guess[...], table.astype(jnp.bfloat16), preferred_element_type=jnp.float32
    )


def turned_kernel(per_mol, dest, info, guess, blocks, label, out, wide, mine, turned, slots):
    step = pl.program_id(0)
    teams = out.shape[0]
    width = SIDES * CAP

    @pl.when(step == 0)
    def _():
        def clear(team, _):
            start = pl.multiple_of(team * width, width)
            for part in range(3):
                slots[part, pl.ds(start, width), :] = jnp.zeros((width, LANES), jnp.float32)
            return 0

        lax.fori_loop(0, teams, clear, 0)

    wide[...] = blocks[...].astype(jnp.float32)
    mine[...] = spread(guess, step * LANES, per_mol, info[1])
    results = []
    for side in range(2):
        sums = [[None] * 3 for _ in range(OCC)]
        for inner in range(BAS):
            first = (side * BAS + inner) * BAS
            block = [wide[first + 8 * g : first + 8 * g + 8, :] for g in range(3)]
            for k in range(OCC):
                row = mine[inner * OCC + k : inner * OCC + k + 1, :]
                for g in range(3):
                    term = block[g] * row
                    sums[k][g] = term if inner == 0 else sums[k][g] + term
        results += [sums[k][g] for k in range(OCC) for g in range(3)]
    for part in range(3):
        turned[part] = jnp.concatenate(results[part * 16 : part * 16 + 16], axis=0).T

    def move(pair, _):
        at = dest[step, pair]
        for part in range(3):
            slots[part, pl.ds(at, 1), :] = turned[part, pl.ds(pair, 1), :]
        return 0

    lax.fori_loop(0, LANES, move, 0, unroll=16)

    @pl.when(step == pl.num_programs(0) - 1)
    def _():
        def finish(team, _):
            start = pl.multiple_of(team * width, width)
            for part in range(3):
                out[team, part * width : (part + 1) * width, :] = slots[
                    part, pl.ds(start, width), :
                ].astype(jnp.bfloat16)
            names = label[pl.ds(pl.multiple_of(team * 8, 8), 8), :]
            names = jnp.concatenate([names, jnp.zeros_like(names)], axis=0)
            out[team, 3 * width : 3 * width + 16, :] = names.astype(jnp.bfloat16)
            return 0

        lax.fori_loop(0, teams, finish, 0)


def apply_blocks(wide, theirs, applied, mine):
    other = [theirs[OCC * b : OCC * b + OCC, :] for b in range(BAS)]
    reduced = [[None] * OCC for _ in range(2)]
    for a in range(BAS):
        for side in range(2):
            first = (side * BAS + a) * BAS
            total = None
            for b in range(BAS):
                term = wide[first + b : first + b + 1, :] * other[b]
                total = term if total is None else total + term
            row = (side * BAS + a) * OCC
            applied[row : row + OCC, :] = total
            if mine is not None:
                for k in range(OCC):
                    term = mine[a * OCC + k : a * OCC + k + 1, :] * total
                    reduced[side][k] = term if a == 0 else reduced[side][k] + term
    return reduced


def diagonal_kernel(guess, blocks, out, wide, mine):
    wide[...] = blocks[...].astype(jnp.float32)
    mine[...] = guess[...].astype(jnp.float32)
    apply_blocks(wide, mine, out, None)


def pairs_kernel(
    per_mol, index, info, guess, blocks, half, local, table, scores, total,
    wide, mine, theirs, applied, near_a, near_b, held, stage, sems,
):
    step = pl.program_id(0)
    chunk = stage.shape[1]
    chunks = table.shape[0] // chunk
    mols = guess.shape[1]

    @pl.when(step == 0)
    def _():
        total[...] = local[...]

        def copy(at):
            return pltpu.make_async_copy(
                table.at[pl.ds(at * chunk, chunk), :], stage.at[at % 2], sems.at[at % 2]
            )

        copy(0).start()
        for at in range(chunks):
            if at + 1 < chunks:
                copy(at + 1).start()
            copy(at).wait()
            held[at * chunk : (at + 1) * chunk, :] = stage[at % 2].astype(jnp.float32)

    def pick(pair, _):
        near_a[pl.ds(pair, 1), :] = held[pl.ds(index[0, step, pair], 1), :]
        near_b[pl.ds(pair, 1), :] = held[pl.ds(index[1, step, pair], 1), :]
        return 0

    lax.fori_loop(0, LANES, pick, 0, unroll=16)
    theirs[:LANES, :] = near_a[...].T
    rest = near_b[...].T
    theirs[LANES:, :] = jnp.where(half[0] > 0, rest[FEAT - LANES :], rest[: FEAT - LANES])
    wide[...] = blocks[...].astype(jnp.float32)
    mine[...] = spread(guess, step * LANES, per_mol, info[1])
    reduced = apply_blocks(wide, theirs, applied, mine)
    scores[...] = jnp.concatenate(reduced[0] + reduced[1], axis=0)
    mol = iota((LANES, mols), 1)
    pair = iota((LANES, mols), 0) + step * LANES
    collapse = (pair >= mol * per_mol) & (pair < (mol + 1) * per_mol) & (mol < info[1])
    total[...] += jnp.dot(
        applied[...].astype(jnp.bfloat16),
        collapse.astype(jnp.bfloat16),
        preferred_element_type=jnp.float32,
    )


def collect_kernel(blocks, lower, here, upper, sums):
    step = pl.program_id(0)
    mols = here.shape[0]
    width = SIDES * CAP

    @pl.when(step == 0)
    def _():
        sums[...] = jnp.zeros_like(sums)

    mol = iota((mols, LANES), 0).astype(jnp.float32)
    names = [blocks[i, 3 * width : 3 * width + 16, :].astype(jnp.float32) for i in range(2)]
    first = iota((1, LANES), 1) < CAP
    for side in range(SIDES):
        name = jnp.where(first, names[0][side : side + 1], names[1][side : side + 1])
        hit = (mol == name).astype(jnp.bfloat16)
        for part in range(3):
            at = part * width + side * CAP
            values = jnp.concatenate([blocks[i, at : at + CAP, :] for i in range(2)], axis=0)
            sums[side, part] += jnp.dot(hit, values, preferred_element_type=jnp.float32)

    @pl.when(step == pl.num_programs(0) - 1)
    def _():
        for part in range(3):
            cut = slice(part * LANES, (part + 1) * LANES)
            lower[:, cut] = sums[0, part].astype(lower.dtype)
            here[:, cut] = sums[1, part]
            upper[:, cut] = sums[2, part].astype(upper.dtype)


def finish_kernel(info, total, here, from_lower, from_upper, out):
    mols = here.shape[0]
    back = here[...] + from_lower[...].astype(jnp.float32) + from_upper[...].astype(jnp.float32)
    high = back.astype(jnp.bfloat16)
    low = (back - high.astype(jnp.float32)).astype(jnp.bfloat16)
    row = iota((ROWS, ROWS), 0)
    column = iota((ROWS, ROWS), 1)
    turn = (column // FEAT) * FEAT + column % BAS * OCC + column % FEAT // BAS
    order = (row == turn).astype(jnp.bfloat16)
    returned = lax.dot_general(order, high, NT, preferred_element_type=jnp.float32)
    returned = returned + lax.dot_general(order, low, NT, preferred_element_type=jnp.float32)
    alive = iota((ROWS, mols), 1) < info[1]
    out[...] = jnp.where(alive, total[...] + returned, 0.0)


def shifted(block, axis, distance):
    devices = range(lax.axis_size(axis))
    route = [((i - distance) % len(devices), i) for i in devices]
    return lax.ppermute(block, axis, route)


def params(mib=48):
    return pltpu.CompilerParams(vmem_limit_bytes=mib * 1024 * 1024)


def on_device(history, diag_blocks, pair_blocks, neighbours, counts):
    mols = history.shape[2]
    pairs = pair_blocks.shape[1]
    per_mol = pairs // mols
    teams = lax.axis_size("sub")
    domains = lax.axis_size("dom")
    columns = pairs // LANES
    held_rows = mols * FEAT // LANES
    width = SIDES * CAP
    shape = jax.ShapeDtypeStruct
    f32, bf16, i32 = jnp.float32, jnp.bfloat16, jnp.int32
    info = jnp.stack([lax.axis_index("dom"), counts[0], lax.axis_index("sub") % 2]).astype(i32)
    guess, rows, dest, index, label = pl.pallas_call(
        functools.partial(prepare_kernel, teams, domains),
        out_shape=(
            shape((FEAT, mols), bf16),
            shape((held_rows, LANES), bf16),
            shape((columns, LANES), i32),
            shape((3, columns, LANES), i32),
            shape((teams * 8, LANES), f32),
        ),
        in_specs=[SMEM, VMEM, VMEM],
        out_specs=(VMEM,) * 5,
        compiler_params=params(),
        name="prepare",
    )(info, history, neighbours.reshape(columns, LANES))

    near = jnp.stack([shifted(rows, "dom", 1), rows, shifted(rows, "dom", -1)])
    table = lax.all_gather(near, "sub", axis=0, tiled=False)
    table = table.reshape(teams * SIDES * held_rows, LANES)

    payload = pl.pallas_call(
        functools.partial(turned_kernel, per_mol),
        grid=(columns,),
        out_shape=shape((teams, 3 * width + 16, LANES), bf16),
        in_specs=[
            SMEM,
            SMEM,
            pl.BlockSpec((FEAT, mols), lambda i: (0, 0)),
            pl.BlockSpec((6 * FEAT, LANES), lambda i: (0, i)),
            pl.BlockSpec((teams * 8, LANES), lambda i: (0, 0)),
        ],
        out_specs=pl.BlockSpec((teams, 3 * width + 16, LANES), lambda i: (0, 0, 0)),
        scratch_shapes=[
            pltpu.VMEM((6 * FEAT, LANES), f32),
            pltpu.VMEM((FEAT, LANES), f32),
            pltpu.VMEM((3, LANES, LANES), f32),
            pltpu.VMEM((3, teams * width, LANES), f32),
        ],
        compiler_params=params(),
        name="turned",
    )(dest, info, guess, pair_blocks, label)

    received = lax.all_to_all(payload, "sub", 0, 0, tiled=True)

    local = pl.pallas_call(
        diagonal_kernel,
        grid=(mols // LANES,),
        out_shape=shape((ROWS, mols), f32),
        in_specs=[
            pl.BlockSpec((FEAT, LANES), lambda i: (0, i)),
            pl.BlockSpec((6 * FEAT, LANES), lambda i: (0, i)),
        ],
        out_specs=pl.BlockSpec((ROWS, LANES), lambda i: (0, i)),
        scratch_shapes=[
            pltpu.VMEM((6 * FEAT, LANES), f32),
            pltpu.VMEM((FEAT, LANES), f32),
        ],
        compiler_params=params(),
        name="diagonal",
    )(guess, diag_blocks)

    chunk = held_rows * SIDES * 2
    scores, total = pl.pallas_call(
        functools.partial(pairs_kernel, per_mol),
        grid=(columns,),
        out_shape=(shape((ROWS // 3, pairs), f32), shape((ROWS, mols), f32)),
        in_specs=[
            SMEM,
            SMEM,
            pl.BlockSpec((FEAT, mols), lambda i: (0, 0)),
            pl.BlockSpec((6 * FEAT, LANES), lambda i: (0, i)),
            pl.BlockSpec((1, 1, LANES), lambda i: (i, 0, 0)),
            pl.BlockSpec((ROWS, mols), lambda i: (0, 0)),
            pl.BlockSpec(memory_space=pl.ANY),
        ],
        out_specs=(
            pl.BlockSpec((ROWS // 3, LANES), lambda i: (0, i)),
            pl.BlockSpec((ROWS, mols), lambda i: (0, 0)),
        ),
        scratch_shapes=[
            pltpu.VMEM((6 * FEAT, LANES), f32),
            pltpu.VMEM((FEAT, LANES), f32),
            pltpu.VMEM((FEAT, LANES), f32),
            pltpu.VMEM((ROWS, LANES), f32),
            pltpu.VMEM((LANES, LANES), f32),
            pltpu.VMEM((LANES, LANES), f32),
            pltpu.VMEM((teams * SIDES * held_rows, LANES), f32),
            pltpu.VMEM((2, chunk, LANES), bf16),
            pltpu.SemaphoreType.DMA((2,)),
        ],
        compiler_params=params(),
        name="pairs",
    )(index, info, guess, pair_blocks, index[2].reshape(columns, 1, LANES), local, table)

    whole = pl.BlockSpec((mols, ROWS), lambda i: (0, 0))
    lower, here, upper = pl.pallas_call(
        collect_kernel,
        grid=(teams // 2,),
        out_shape=(shape((mols, ROWS), bf16), shape((mols, ROWS), f32), shape((mols, ROWS), bf16)),
        in_specs=[pl.BlockSpec((2, 3 * width + 16, LANES), lambda i: (i, 0, 0))],
        out_specs=(whole,) * 3,
        scratch_shapes=[pltpu.VMEM((SIDES, 3, mols, LANES), f32)],
        compiler_params=params(),
        name="collect",
    )(received)

    products = pl.pallas_call(
        finish_kernel,
        out_shape=shape((ROWS, mols), f32),
        in_specs=[SMEM] + [VMEM] * 4,
        out_specs=VMEM,
        compiler_params=params(),
        name="finish",
    )(info, total, here, shifted(upper, "dom", 1), shifted(lower, "dom", -1))
    return products, scores


def solution(mesh):
    in_specs = (
        P(None, None, ("dom", "sub")),
        P(None, ("dom", "sub")),
        P(None, ("dom", "sub")),
        P(("dom", "sub")),
        P(("dom", "sub")),
    )
    out_specs = (P(None, ("dom", "sub")), P(None, ("dom", "sub")))
    return jax.shard_map(
        on_device, mesh=mesh, in_specs=in_specs, out_specs=out_specs, check_vma=False
    )
```

time: 567 us -> 189 us (0.33)
  waiting for transfers between devices: 212 us -> 2.64 us
  other arithmetic: 192 us -> 0.83 us
  local copies, waits for them, and re-layouts: 130 us -> 1.85 us
  blocking collectives: 0 us -> 85.3 us
  Pallas kernels: 0 us -> 75.6 us
    reduce_scatter x1 -> x0, waiting for transfers between devices: 162 us -> none  [on_device(): summed = lax.psum_scatter(back, 'sub', scatter_dimension=2, tiled=True)]
    mul x48 -> x0, other arithmetic: 112 us -> none  [the longest x28 40 us: pair_terms(): square[:, :, inner, None, :].astype(jnp.float32) * other[None, None, inner]]
    all_to_all x0 -> x1, blocking collectives: none -> 85.3 us  [on_device(): received = lax.all_to_all(payload, 'sub', 0, 0, tiled=True)]
    pallas_call x0 -> x6, Pallas kernels: none -> 75.6 us  [the longest x1 39.1 us: on_device(): pl.pallas_call(functools.partial(pairs_kernel, per_mol), grid=(columns,),...]
    ppermute x2 -> x0, waiting for transfers between devices: 47.1 us -> none  [the longest x1 47.1 us: with_halo(): lax.ppermute(lax.slice_in_dim(block, block.shape[dim] - width, None, axis...]
    reshape x1 -> x0, local copies, waits for them, and re-layouts: 36.9 us -> none  [on_device(): back = back.reshape(rows, 3, teams * mols)]
    slice x5 -> x1, local copies, waits for them, and re-layouts: 36.9 us -> 0.01 us  [on_device(): index[2].reshape(columns, 1, LANES)]
    scatter-add x1 -> x0, other arithmetic: 34.1 us -> none  [on_device(): jnp.zeros((rows, 3 * teams * mols), jnp.float32).at[:, target].add(sent)]
  transfers between devices with their start and end apart: 6 -> 5, of which waited for: 4 -> 1; matrix products, arithmetic and copies ran while one was open for 21% -> 0% of each run, Pallas kernels for 0% -> 38%
where the time goes in v1:
time: 189 us; the launch traced here: 186 us
  blocking collectives  85.3 us (45%)
  Pallas kernels  75.6 us (40%)
  between operations  14.8 us (8%)
  starting transfers between devices  5.44 us (3%)
  waiting for transfers between devices  2.64 us (1%)
    all_to_all x1, blocking collectives, on_device(): received = lax.all_to_all(payload, 'sub', 0, 0, tiled=True)  85.3 us
    pallas_call x1, Pallas kernels, on_device(): pl.pallas_call(functools.partial(pairs_kernel, per_mol), grid=(columns,),...  39.1 us
    pallas_call x1, Pallas kernels, on_device(): pl.pallas_call(functools.partial(turned_kernel, per_mol), grid=(columns,)...  25.5 us
    ppermute x4, starting transfers between devices, shifted(): return lax.ppermute(block, axis, route)  5.4 us
    pallas_call x1, Pallas kernels, on_device(): pl.pallas_call(collect_kernel, grid=(teams // 2,), out_shape=(shape((mols...  5.23 us
  transfers between devices with their start and end apart: 5, of which 1 were waited for; matrix products, arithmetic and copies ran while one was open for 0% of the time, Pallas kernels for 38%

profile of v1, /device:TPU:6, one launch (start us, length us, event | category | flops | bytes accessed | tf_op | source)
XLA Modules:
  0.0 186.4 jit_solution(15070074924143045842)
XLA Ops:
  7.2 0.0 all-gather.3.cloned.1.call-start
  7.9 0.1 pad_add_fusion.info
  7.9 0.0 copy-start
  7.9 1.1 copy-done
  9.1 0.7 copy-done.2
  9.8 3.0 %prepare.1 = (bf16[192,256]{1,0:T(8,128)(2,1)S(1)}, bf16[384,128]{1,0:T(8,128)(2,1)S(1)}, s32[24,128]{1,0:T(8,128)S(1)}, s32[3,24,128]{2,1,0:T(8,128)S(1)}, f32[256,128]{1,0:T(8,128)S(1)}) custom-call(s32[3]{0:T(128)S(1)} %pad_add_fusion.info, f32[4,192,256]{2,1,0:T(8,128)S(1)} %copy-done, s32[24,128]{1,0:T(8,128)S(1)} %bitcast.10), custom_call_target="tpu_custom_call" | custom-call | tf_op jit(solution)/shard_map/prepare/pallas_call | solution.py:284
  12.8 0.9 collective-permute-start.1
  13.7 2.4 %collective-permute-start = (bf16[384,128]{1,0:T(8,128)(2,1)S(1)}, bf16[384,128]{1,0:T(8,128)(2,1)S(1)}, u32[]{:S(2)}, u32[]{:S(2)}) collective-permute-start(bf16[384,128]{1,0:T(8,128)(2,1)S(1)} %get-tuple-element.14), channel_id=1, source_target_pairs={{96,0},{0,32},{32,64},{64,96},{97,1},{1,33},{33,65},{65,97},{98,2}... | collective-permute-start | bytes 294920 | tf_op jit(solution)/shard_map/ppermute | solution.py:265
  16.1 2.6 %collective-permute-done.1 = bf16[384,128]{1,0:T(8,128)(2,1)S(1)} collective-permute-done((bf16[384,128]{1,0:T(8,128)(2,1)S(1)}, bf16[384,128]{1,0:T(8,128)(2,1)S(1)}, u32[]{:S(2)}, u32[]{:S(2)}) %collective-permute-start.1) | collective-permute-done | bytes 98336 | tf_op jit(solution)/shard_map/ppermute | solution.py:265
  18.7 0.0 collective-permute-done
  18.7 0.7 pad_maximum_fusion
  19.4 0.0 all-gather.3.cloned.1.call-update
  19.5 25.5 %turned.1 = bf16[32,592,128]{2,1,0:T(8,128)(2,1)S(1)} custom-call(s32[24,128]{1,0:T(8,128)S(1)} %get-tuple-element.16.dest, s32[3]{0:T(128)S(1)} %pad_add_fusion.info, bf16[192,256]{1,0:T(8,128)(2,1)S(1)} %get-tuple-element.13.guess, bf16[1152,3072]{1,0:T(8,128)(2,1)} %blocks.5, f32[256,128]{1,0:T(8,128)S(1)} %get-tuple-element.17.label), custom_call_target="tpu_custom_call" | custom-call | tf_op jit(solution)/shard_map/turned/pallas_call | solution.py:303
  45.0 85.3 %all_to_all.5.blocks = bf16[32,592,128]{2,1,0:T(8,128)(2,1)S(1)} all-to-all(bf16[32,592,128]{2,1,0:T(8,128)(2,1)S(1)} %turned.1), channel_id=1, replica_groups=mesh['dom'=4,'sub'=32] {'sub'}, dimensions={0} | all-to-all | bytes 9699328 | tf_op jit(solution)/shard_map/all_to_all | solution.py:325
  130.3 5.2 %collect.1 = (bf16[256,384]{1,0:T(8,128)(2,1)S(1)}, f32[256,384]{1,0:T(8,128)S(1)}, bf16[256,384]{1,0:T(8,128)(2,1)S(1)}) custom-call(bf16[32,592,128]{2,1,0:T(8,128)(2,1)S(1)} %all_to_all.5.blocks), custom_call_target="tpu_custom_call" | custom-call | tf_op jit(solution)/shard_map/collect/pallas_call | solution.py:378
  135.5 0.6 collective-permute-start.2
  136.1 1.5 collective-permute-start.3
  137.6 0.0 copy-done.1
  137.6 1.0 diagonal.1.local
  138.6 0.0 all-gather.3.cloned.1.call-done
  138.6 39.1 %pairs.1 = (f32[128,3072]{1,0:T(8,128)}, f32[384,256]{1,0:T(8,128)S(1)}) custom-call(s32[3,24,128]{2,1,0:T(8,128)S(1)} %get-tuple-element.12.index, s32[3]{0:T(128)S(1)} %pad_add_fusion.info, bf16[192,256]{1,0:T(8,128)(2,1)S(1)} %get-tuple-element.13.guess, bf16[1152,3072]{1,0:T(8,128)(2,1)} %blocks.5, s32[24,1,128]{2,1,0:T(1,128)S(1)} %bitcast.9, ...), custom_call_target="tpu_custom_call" | custom-call | tf_op jit(solution)/shard_map/pairs/pallas_call | solution.py:345
  177.8 0.0 collective-permute-done.2.from_lower
  177.8 0.0 collective-permute-done.3.from_upper
  177.8 1.7 finish.1
  (3 shorter events, 0.0 us)
Async XLA Ops:
  7.2 131.5 %all-gather.3.cloned.1.call-start = ((), (), s32[]{:S(2)}) async-start(), calls=%async_computation.1 | async-start | bytes 9732096 | tf_op jit(solution)/shard_map/all_gather | solution.py:300
  7.9 1.1 copy-start
  9.1 0.7 copy-start.2
  12.8 5.9 %collective-permute-start.1 = (bf16[384,128]{1,0:T(8,128)(2,1)S(1)}, bf16[384,128]{1,0:T(8,128)(2,1)S(1)}, u32[]{:S(2)}, u32[]{:S(2)}) collective-permute-start(bf16[384,128]{1,0:T(8,128)(2,1)S(1)} %get-tuple-element.14), channel_id=1, source_target_pairs={{32,0},{64,32},{96,64},{0,96},{33,1},{65,33},{97,65},{1,97},{34,2}... | collective-permute-start | bytes 294920 | tf_op jit(solution)/shard_map/ppermute | solution.py:265
  13.7 5.0 %collective-permute-start = (bf16[384,128]{1,0:T(8,128)(2,1)S(1)}, bf16[384,128]{1,0:T(8,128)(2,1)S(1)}, u32[]{:S(2)}, u32[]{:S(2)}) collective-permute-start(bf16[384,128]{1,0:T(8,128)(2,1)S(1)} %get-tuple-element.14), channel_id=1, source_target_pairs={{96,0},{0,32},{32,64},{64,96},{97,1},{1,33},{33,65},{65,97},{98,2}... | collective-permute-start | bytes 294920 | tf_op jit(solution)/shard_map/ppermute | solution.py:265
  130.3 7.3 %copy-start.1 = (bf16[1152,256]{1,0:T(8,128)(2,1)S(1)}, bf16[1152,256]{1,0:T(8,128)(2,1)}, u32[]{:S(2)}) copy-start(bf16[1152,256]{1,0:T(8,128)(2,1)} %blocks.3) | copy-start | bytes 1769476
  135.5 42.3 %collective-permute-start.2 = (bf16[256,384]{1,0:T(8,128)(2,1)S(1)}, bf16[256,384]{1,0:T(8,128)(2,1)S(1)}, u32[]{:S(2)}, u32[]{:S(2)}) collective-permute-start(bf16[256,384]{1,0:T(8,128)(2,1)S(1)} %get-tuple-element.19), channel_id=1, source_target_pairs={{96,0},{0,32},{32,64},{64,96},{97,1},{1,33},{33,65},{65,97},{98,2}... | collective-permute-start | bytes 589832 | tf_op jit(solution)/shard_map/ppermute | solution.py:265
  136.1 41.7 %collective-permute-start.3 = (bf16[256,384]{1,0:T(8,128)(2,1)S(1)}, bf16[256,384]{1,0:T(8,128)(2,1)S(1)}, u32[]{:S(2)}, u32[]{:S(2)}) collective-permute-start(bf16[256,384]{1,0:T(8,128)(2,1)S(1)} %get-tuple-element.20), channel_id=1, source_target_pairs={{32,0},{64,32},{96,64},{0,96},{33,1},{65,33},{97,65},{1,97},{34,2}... | collective-permute-start | bytes 589832 | tf_op jit(solution)/shard_map/ppermute | solution.py:265
Sparse Core Ops, SparseCore 0:
  19.6 104.2 all-gather.2

commit v2 on v1

v2 whole, which is shorter than its diff:
```python
import functools

import jax
import jax.numpy as jnp
from jax import lax
from jax.experimental import pallas as pl
from jax.experimental.pallas import tpu as pltpu
from jax.sharding import PartitionSpec as P

BAS = 24
OCC = 8
FEAT = BAS * OCC
ROWS = 2 * FEAT
CAP = 64
LANES = 128
BLOCK = 4 * LANES
BATCH = 64
SIDES = 3
RING = 4
KEYS = 4
ASPC_WEIGHTS = (2.8, -2.8, 1.2, -0.2)
VMEM = pl.BlockSpec(memory_space=pltpu.VMEM)
SMEM = pl.BlockSpec(memory_space=pltpu.SMEM)
NT = (((1,), (1,)), ((), ()))
WIDTH = SIDES * CAP
PACKED = CAP * FEAT // LANES


def iota(shape, dim):
    return lax.broadcasted_iota(jnp.int32, shape, dim)


def relative(team, me):
    z = (team // (2 * RING) - me // (2 * RING) + RING) % RING
    y = (team // 2 % RING - me // 2 % RING + RING) % RING
    return (team % 2 + me) % 2 * RING * RING + y * RING + z


def absolute(place, me):
    z = (place + me // (2 * RING)) % RING
    y = (place // RING + me // 2) % RING
    return (z * RING + y) * 2 + (place // (RING * RING) + me) % 2


def ahead(block, dz, dy, core):
    route = []
    for target in range(2 * RING * RING):
        z, y, c = target // (2 * RING), target // 2 % RING, target % 2
        source = ((z + dz) % RING * RING + (y + dy) % RING) * 2 + (c + core) % 2
        route.append((source, target))
    return lax.ppermute(block, "sub", route)


def predict_kernel(history, guess, rows):
    mols = guess.shape[1]
    total = ASPC_WEIGHTS[0] * history[0]
    for level in range(1, 4):
        total = total + ASPC_WEIGHTS[level] * history[level]
    rounded = total.astype(jnp.bfloat16)
    guess[...] = rounded
    wide = rounded.astype(jnp.float32)
    for part in range(mols // LANES):
        cut = slice(part * LANES, (part + 1) * LANES)
        rows[cut, :] = wide[:LANES, cut].T.astype(jnp.bfloat16)
    rest = jnp.concatenate([wide[LANES:, :LANES], wide[LANES:, LANES:]], axis=0)
    rows[mols:, :] = rest.T.astype(jnp.bfloat16)


def rank_kernel(
    teams, domains, mols, info, near, dest, first_rows, rest_rows, half, wanted, label
):
    my_domain = info[0]
    parity = info[2]
    listed = near[...]
    owner = listed // mols
    slot = listed % mols
    team = relative(owner % teams, info[3])
    offset = (owner // teams - my_domain + 1 + domains) % domains
    place = team * WIDTH + offset * CAP
    inside = offset == 1
    held_rows = mols * FEAT // LANES
    beyond = teams * held_rows + (offset // 2 * teams + team) * PACKED
    key = team * KEYS + offset
    keys = teams * KEYS
    square = (LANES, 2 * LANES)
    before = ((iota(square, 0) < iota(square, 1)) | (iota(square, 1) >= LANES)).astype(jnp.bfloat16)
    which = iota((keys, LANES), 0)
    carry = jnp.zeros((keys, LANES), jnp.float32)
    names = jnp.zeros((keys, LANES), jnp.float32)
    for block in range(listed.shape[0]):
        at = slice(block, block + 1)
        hit = which == key[at]
        ones = jnp.where(hit, 1.0, 0.0)
        sums = jnp.dot(ones.astype(jnp.bfloat16), before, preferred_element_type=jnp.float32)
        prior = sums[:, :LANES] + carry
        carry = carry + sums[:, LANES:]
        rank = jnp.sum(jnp.where(hit, prior, 0.0), axis=0, keepdims=True).astype(jnp.int32)
        dest[at, :] = place[at] + rank
        base = team[at] * held_rows
        first_rows[at, :] = jnp.where(inside[at], base + slot[at], beyond[at] + rank)
        rest_rows[at, :] = jnp.where(
            inside[at],
            base + mols + slot[at] % LANES,
            beyond[at] + CAP + rank % (CAP // 2),
        )
        half[at, :] = jnp.where(inside[at], slot[at] // LANES, rank // (CAP // 2))
        column = iota((LANES, LANES), 0) == rank
        named = jnp.where(hit, slot[at].astype(jnp.float32), 0.0)
        names = names + lax.dot_general(
            named.astype(jnp.bfloat16),
            column.astype(jnp.bfloat16),
            NT,
            preferred_element_type=jnp.float32,
        )
    wanted[...] = names.astype(jnp.int32)
    label[...] = jnp.where(parity == 1, pltpu.roll(names, CAP, 1), names)


def answer_kernel(from_lower, from_upper, same, other, to_lower, to_upper):
    count, held_rows = same.shape[:2]
    teams = 2 * count
    mols = held_rows * LANES // FEAT
    half = CAP // 2
    names = []
    for asked in (from_lower, from_upper):
        names.append(asked[...].astype(jnp.float32).T)
    low = iota((LANES, LANES), 1) < FEAT - LANES
    mol = iota((CAP, mols), 1).astype(jnp.float32)
    for team in range(teams):
        held, at = (same, team) if team < count else (other, team - count)
        packed = held[at, mols:, :].astype(jnp.float32)
        turned = pltpu.roll(packed, FEAT - LANES, 1)
        rest = jnp.concatenate([jnp.where(low, packed, turned), jnp.where(low, turned, packed)], axis=0)
        values = jnp.concatenate([held[at, :mols, :], rest.astype(jnp.bfloat16)], axis=1)
        hits = []
        for side in range(2):
            column = team * KEYS + 2 - 2 * side
            name = names[side][:CAP, column : column + 1]
            hits.append((name == mol).astype(jnp.bfloat16))
        found = jnp.dot(jnp.concatenate(hits, axis=0), values, preferred_element_type=jnp.float32)
        for side, out in enumerate((to_lower, to_upper)):
            mine = found[side * CAP : (side + 1) * CAP]
            out[team, :CAP, :] = mine[:, :LANES].astype(jnp.bfloat16)
            pair = jnp.where(low[:half], mine[:half, LANES:], mine[half:, LANES:])
            out[team, CAP:, :] = pair.astype(jnp.bfloat16)


def owners(mols, first, per_mol, count):
    mol = (iota((1, BLOCK), 1) + first) // per_mol
    mol = jnp.where(mol < count, mol, -1)
    return (iota((mols, BLOCK), 0) == mol).astype(jnp.bfloat16)


def turned_kernel(per_mol, dest, info, guess, blocks, label, out, wide, mine, turned, slots, stage, sems):
    step = pl.program_id(0)
    teams = out.shape[0]
    width = WIDTH

    @pl.when(step == 0)
    def _():
        def clear(team, _):
            start = pl.multiple_of(team * width, width)
            for part in range(3):
                slots[part, pl.ds(start, width), :] = jnp.zeros((width, LANES), jnp.float32)
            return 0

        lax.fori_loop(0, teams, clear, 0)

    table = owners(guess.shape[1], step * BLOCK, per_mol, info[1])
    mine[...] = jnp.dot(guess[...], table, preferred_element_type=jnp.float32)

    def column(at, _):
        cut = pl.ds(pl.multiple_of(at * LANES, LANES), LANES)
        wide[...] = blocks[:, cut].astype(jnp.float32)
        results = []
        for side in range(2):
            sums = [[None] * 3 for _ in range(OCC)]
            for inner in range(BAS):
                first = (side * BAS + inner) * BAS
                block = [wide[first + 8 * g : first + 8 * g + 8, :] for g in range(3)]
                for k in range(OCC):
                    row = mine[inner * OCC + k : inner * OCC + k + 1, cut]
                    for g in range(3):
                        term = block[g] * row
                        sums[k][g] = term if inner == 0 else sums[k][g] + term
            results += [sums[k][g] for k in range(OCC) for g in range(3)]
        for part in range(3):
            turned[part] = jnp.concatenate(results[part * 16 : part * 16 + 16], axis=0).T

        line = step * BLOCK + at * LANES

        def move(first, _):
            first = pl.multiple_of(first * BATCH, BATCH)
            places = [dest[line + first + i] for i in range(BATCH)]
            rows = [
                [turned[part, pl.ds(first + i, 1), :] for part in range(3)] for i in range(BATCH)
            ]
            for place, row in zip(places, rows):
                for part in range(3):
                    slots[part, pl.ds(place, 1), :] = row[part]
            return 0

        return lax.fori_loop(0, LANES // BATCH, move, 0)

    lax.fori_loop(0, BLOCK // LANES, column, 0)

    @pl.when(step == pl.num_programs(0) - 1)
    def _():
        def copy(team):
            return pltpu.make_async_copy(
                stage.at[team], out.at[absolute(team, info[3])], sems.at[team]
            )

        def finish(team, _):
            start = pl.multiple_of(team * width, width)
            for part in range(3):
                stage[team, part * width : (part + 1) * width, :] = slots[
                    part, pl.ds(start, width), :
                ].astype(jnp.bfloat16)
            names = label[pl.ds(pl.multiple_of(team // 2 * 8, 8), 8), :]
            names = jnp.where(team % 2 == 1, pltpu.roll(names, KEYS, 0), names)
            names = jnp.concatenate([names, jnp.zeros_like(names)], axis=0)
            stage[team, 3 * width :, :] = names.astype(jnp.bfloat16)
            copy(team).start()
            return 0

        def wait(team, _):
            copy(team).wait()
            return 0

        lax.fori_loop(0, teams, finish, 0)
        lax.fori_loop(0, teams, wait, 0)


def apply_blocks(wide, theirs, applied, mine, cut):
    other = [theirs[OCC * b : OCC * b + OCC, :] for b in range(BAS)]
    reduced = [[None] * OCC for _ in range(2)]
    for a in range(BAS):
        for side in range(2):
            first = (side * BAS + a) * BAS
            total = None
            for b in range(BAS):
                term = wide[first + b : first + b + 1, :] * other[b]
                total = term if total is None else total + term
            row = (side * BAS + a) * OCC
            applied[row : row + OCC, cut] = total
            if mine is not None:
                for k in range(OCC):
                    term = mine[a * OCC + k : a * OCC + k + 1, cut] * total
                    reduced[side][k] = term if a == 0 else reduced[side][k] + term
    return reduced


def diagonal_kernel(guess, blocks, out, wide, mine):
    wide[...] = blocks[...].astype(jnp.float32)
    mine[...] = guess[...].astype(jnp.float32)
    apply_blocks(wide, mine, out, None, slice(0, LANES))


def pairs_kernel(
    per_mol, first_rows, rest_rows, info, guess, blocks, half, local, same, other, lower, upper, scores, total,
    wide, mine, theirs, applied, near_a, near_b, held,
):
    step = pl.program_id(0)
    mols = guess.shape[1]

    @pl.when(step == 0)
    def _():
        total[...] = local[...]

        base = 0
        for source in (same, other, lower, upper):
            rows = source.shape[1]

            def widen(team, _):
                start = pl.multiple_of(base + team * rows, rows)
                held[pl.ds(start, rows), :] = source[team].astype(jnp.float32)
                return 0

            lax.fori_loop(0, source.shape[0], widen, 0)
            base += source.shape[0] * rows

    table = owners(mols, step * BLOCK, per_mol, info[1])
    mine[...] = jnp.dot(guess[...], table, preferred_element_type=jnp.float32)

    def column(at, _):
        cut = pl.ds(pl.multiple_of(at * LANES, LANES), LANES)
        line = step * (BLOCK // LANES) + at

        def pick(first, _):
            first = pl.multiple_of(first * BATCH, BATCH)
            for index, near in ((first_rows, near_a), (rest_rows, near_b)):
                places = [index[line * LANES + first + i] for i in range(BATCH)]
                rows = [held[pl.ds(place, 1), :] for place in places]
                near[pl.ds(first, BATCH), :] = jnp.concatenate(rows, axis=0)
            return 0

        lax.fori_loop(0, LANES // BATCH, pick, 0)
        theirs[:LANES, :] = near_a[...].T
        rest = near_b[...].T
        theirs[LANES:, :] = jnp.where(
            half[pl.ds(line, 1), :] > 0, rest[FEAT - LANES :], rest[: FEAT - LANES]
        )
        wide[...] = blocks[:, cut].astype(jnp.float32)
        reduced = apply_blocks(wide, theirs, applied, mine, cut)
        scores[:, cut] = jnp.concatenate(reduced[0] + reduced[1], axis=0)
        return 0

    lax.fori_loop(0, BLOCK // LANES, column, 0)
    total[...] += lax.dot_general(
        applied[...].astype(jnp.bfloat16), table, NT, preferred_element_type=jnp.float32
    )


def collect_kernel(blocks, lower, here, upper, sums):
    step = pl.program_id(0)
    mols = here.shape[0]
    group = blocks.shape[0]

    @pl.when(step == 0)
    def _():
        sums[...] = jnp.zeros_like(sums)

    mol = iota((mols, group * CAP), 0).astype(jnp.float32)
    first = iota((1, LANES), 1) < CAP
    labels = [blocks[i, 3 * WIDTH :, :].astype(jnp.float32) for i in range(group)]
    for side in range(SIDES):
        at = slice(side, side + 1)
        names = [jnp.where(first, labels[i][at], labels[i + 1][at]) for i in range(0, group, 2)]
        hit = (mol == jnp.concatenate(names, axis=1)).astype(jnp.bfloat16)
        values = []
        for part in range(3):
            row = part * WIDTH + side * CAP
            values.append(
                jnp.concatenate([blocks[i, row : row + CAP, :] for i in range(group)], axis=0)
            )
        sums[side] += jnp.dot(
            hit, jnp.concatenate(values, axis=1), preferred_element_type=jnp.float32
        )

    @pl.when(step == pl.num_programs(0) - 1)
    def _():
        for side, out in enumerate((lower, here, upper)):
            out[...] = sums[side].astype(out.dtype)


def finish_kernel(info, total, here, from_lower, from_upper, out):
    mols = here.shape[0]
    back = here[...] + from_lower[...].astype(jnp.float32) + from_upper[...].astype(jnp.float32)
    high = back.astype(jnp.bfloat16)
    low = (back - high.astype(jnp.float32)).astype(jnp.bfloat16)
    row = iota((ROWS, ROWS), 0)
    column = iota((ROWS, ROWS), 1)
    turn = (column // FEAT) * FEAT + column % BAS * OCC + column % FEAT // BAS
    order = (row == turn).astype(jnp.bfloat16)
    returned = lax.dot_general(order, high, NT, preferred_element_type=jnp.float32)
    returned = returned + lax.dot_general(order, low, NT, preferred_element_type=jnp.float32)
    alive = iota((ROWS, mols), 1) < info[1]
    out[...] = jnp.where(alive, total[...] + returned, 0.0)


def shifted(block, axis, distance):
    devices = range(lax.axis_size(axis))
    route = [((i - distance) % len(devices), i) for i in devices]
    return lax.ppermute(block, axis, route)


def params(mib=48):
    return pltpu.CompilerParams(vmem_limit_bytes=mib * 1024 * 1024)


def cost(us):
    return pl.CostEstimate(flops=0, transcendentals=0, bytes_accessed=us * 3_600_000)


def on_device(history, diag_blocks, pair_blocks, neighbours, counts):
    mols = history.shape[2]
    pairs = pair_blocks.shape[1]
    per_mol = pairs // mols
    teams = lax.axis_size("sub")
    domains = lax.axis_size("dom")
    columns = pairs // LANES
    held_rows = mols * FEAT // LANES
    shape = jax.ShapeDtypeStruct
    f32, bf16, i32 = jnp.float32, jnp.bfloat16, jnp.int32
    info = jnp.stack([lax.axis_index("dom"), counts[0], lax.axis_index("sub") % 2, lax.axis_index("sub")]).astype(i32)
    guess, rows = pl.pallas_call(
        predict_kernel,
        out_shape=(shape((FEAT, mols), bf16), shape((held_rows, LANES), bf16)),
        in_specs=[VMEM],
        out_specs=(VMEM,) * 2,
        compiler_params=params(),
        name="predict",
    )(history)

    table = shape((columns, LANES), i32)
    dest, first_rows, rest_rows, half, wanted, label = pl.pallas_call(
        functools.partial(rank_kernel, teams, domains, mols),
        out_shape=(table,) * 4 + (shape((teams * KEYS, LANES), i32), shape((teams * KEYS, LANES), f32)),
        in_specs=[SMEM, VMEM],
        out_specs=(VMEM,) * 6,
        compiler_params=params(),
        cost_estimate=cost(3),
        name="rank",
    )(info, neighbours.reshape(columns, LANES))
    dest, first_rows, rest_rows = (x.reshape(pairs) for x in (dest, first_rows, rest_rows))

    same = jnp.stack([rows] + [ahead(rows, z, 0, 0) for z in range(1, RING)])
    same, dest = lax.optimization_barrier((same, dest))
    same = jnp.concatenate([same] + [ahead(same, 0, y, 0) for y in range(1, RING)])
    asked_lower, asked_upper = shifted(wanted, "dom", 1), shifted(wanted, "dom", -1)

    payload = pl.pallas_call(
        functools.partial(turned_kernel, per_mol),
        grid=(pairs // BLOCK,),
        out_shape=shape((teams, 3 * WIDTH + 16, LANES), bf16),
        in_specs=[
            SMEM,
            SMEM,
            pl.BlockSpec((FEAT, mols), lambda i: (0, 0)),
            pl.BlockSpec((6 * FEAT, BLOCK), lambda i: (0, i)),
            pl.BlockSpec((teams * KEYS, LANES), lambda i: (0, 0)),
        ],
        out_specs=pl.BlockSpec(memory_space=pltpu.HBM),
        scratch_shapes=[
            pltpu.VMEM((6 * FEAT, LANES), f32),
            pltpu.VMEM((FEAT, BLOCK), f32),
            pltpu.VMEM((3, LANES, LANES), f32),
            pltpu.VMEM((3, teams * WIDTH, LANES), f32),
            pltpu.VMEM((teams, 3 * WIDTH + 16, LANES), bf16),
            pltpu.SemaphoreType.DMA((teams,)),
        ],
        compiler_params=params(60),
        cost_estimate=cost(25),
        name="turned",
    )(dest, info, guess, pair_blocks, label)

    payload, same = lax.optimization_barrier((payload, same))
    received = lax.all_to_all(payload, "sub", 0, 0, tiled=True)

    other = ahead(same, 0, 0, 1)
    to_lower, to_upper = pl.pallas_call(
        answer_kernel,
        out_shape=(shape((teams, PACKED, LANES), bf16),) * 2,
        in_specs=[VMEM] * 4,
        out_specs=(VMEM,) * 2,
        compiler_params=params(),
        name="answer",
    )(asked_lower, asked_upper, same, other)
    upper = shifted(to_lower, "dom", -1)
    lower = shifted(to_upper, "dom", 1)

    local = pl.pallas_call(
        diagonal_kernel,
        grid=(mols // LANES,),
        out_shape=shape((ROWS, mols), f32),
        in_specs=[
            pl.BlockSpec((FEAT, LANES), lambda i: (0, i)),
            pl.BlockSpec((6 * FEAT, LANES), lambda i: (0, i)),
        ],
        out_specs=pl.BlockSpec((ROWS, LANES), lambda i: (0, i)),
        scratch_shapes=[
            pltpu.VMEM((6 * FEAT, LANES), f32),
            pltpu.VMEM((FEAT, LANES), f32),
        ],
        compiler_params=params(),
        name="diagonal",
    )(guess, diag_blocks)

    scores, total = pl.pallas_call(
        functools.partial(pairs_kernel, per_mol),
        grid=(pairs // BLOCK,),
        out_shape=(shape((ROWS // 3, pairs), f32), shape((ROWS, mols), f32)),
        in_specs=[
            SMEM,
            SMEM,
            SMEM,
            pl.BlockSpec((FEAT, mols), lambda i: (0, 0)),
            pl.BlockSpec((6 * FEAT, BLOCK), lambda i: (0, i)),
            pl.BlockSpec((columns, LANES), lambda i: (0, 0)),
            pl.BlockSpec((ROWS, mols), lambda i: (0, 0)),
            pl.BlockSpec((teams // 2, held_rows, LANES), lambda i: (0, 0, 0)),
            pl.BlockSpec((teams // 2, held_rows, LANES), lambda i: (0, 0, 0)),
            pl.BlockSpec((teams, PACKED, LANES), lambda i: (0, 0, 0)),
            pl.BlockSpec((teams, PACKED, LANES), lambda i: (0, 0, 0)),
        ],
        out_specs=(
            pl.BlockSpec((ROWS // 3, BLOCK), lambda i: (0, i)),
            pl.BlockSpec((ROWS, mols), lambda i: (0, 0)),
        ),
        scratch_shapes=[
            pltpu.VMEM((6 * FEAT, LANES), f32),
            pltpu.VMEM((FEAT, BLOCK), f32),
            pltpu.VMEM((FEAT, LANES), f32),
            pltpu.VMEM((ROWS, BLOCK), f32),
            pltpu.VMEM((LANES, LANES), f32),
            pltpu.VMEM((LANES, LANES), f32),
            pltpu.VMEM((teams * (held_rows + 2 * PACKED), LANES), f32),
        ],
        compiler_params=params(),
        cost_estimate=cost(35),
        name="pairs",
    )(first_rows, rest_rows, info, guess, pair_blocks, half, local, same, other, lower, upper)

    received, total = lax.optimization_barrier((received, total))
    whole = pl.BlockSpec((mols, ROWS), lambda i: (0, 0))
    group = 8
    below, here, above = pl.pallas_call(
        collect_kernel,
        grid=(teams // group,),
        out_shape=(shape((mols, ROWS), bf16), shape((mols, ROWS), f32), shape((mols, ROWS), bf16)),
        in_specs=[pl.BlockSpec((group, 3 * WIDTH + 16, LANES), lambda i: (i, 0, 0))],
        out_specs=(whole,) * 3,
        scratch_shapes=[pltpu.VMEM((SIDES, mols, ROWS), f32)],
        compiler_params=params(),
        name="collect",
    )(received)
    from_lower, from_upper = shifted(above, "dom", 1), shifted(below, "dom", -1)

    products = pl.pallas_call(
        finish_kernel,
        out_shape=shape((ROWS, mols), f32),
        in_specs=[SMEM] + [VMEM] * 4,
        out_specs=VMEM,
        compiler_params=params(),
        name="finish",
    )(info, total, here, from_lower, from_upper)
    return products, scores


def solution(mesh):
    in_specs = (
        P(None, None, ("dom", "sub")),
        P(None, ("dom", "sub")),
        P(None, ("dom", "sub")),
        P(("dom", "sub")),
        P(("dom", "sub")),
    )
    out_specs = (P(None, ("dom", "sub")), P(None, ("dom", "sub")))
    return jax.shard_map(
        on_device, mesh=mesh, in_specs=in_specs, out_specs=out_specs, check_vma=False
    )
```

time: 189 us -> 121 us (0.64); the launches traced: 186 us -> 120 us
  blocking collectives: 85.3 us -> 0 us
  waiting for transfers between devices: 2.64 us -> 34 us
  starting transfers between devices: 5.44 us -> 26 us
  Pallas kernels: 75.6 us -> 55.7 us
  between operations: 14.8 us -> 1.43 us
    all_to_all x1 -> x0, blocking collectives: 85.3 us -> none  [on_device(): received = lax.all_to_all(payload, 'sub', 0, 0, tiled=True)]
    ppermute x4 -> x6, waiting for transfers between devices: 2.6 us -> 26.3 us  [shifted(): return lax.ppermute(block, axis, route)]
    pallas_call x4 -> x6, Pallas kernels: 72.9 us -> 52.9 us  [the longest x1 23.7 us: on_device(): pl.pallas_call(functools.partial(pairs_kernel, per_mol), grid=(pairs // B...]
    ppermute x0 -> x7, starting transfers between devices: none -> 12.5 us  [ahead(): return lax.ppermute(block, 'sub', route)]
    all_to_all x0 -> x1, waiting for transfers between devices: none -> 7.54 us  [on_device(): received = lax.all_to_all(payload, 'sub', 0, 0, tiled=True)]
    all_to_all x0 -> x1, starting transfers between devices: none -> 4.87 us  [on_device(): received = lax.all_to_all(payload, 'sub', 0, 0, tiled=True)]
    ppermute x4 -> x6, starting transfers between devices: 5.4 us -> 8.59 us  [shifted(): return lax.ppermute(block, axis, route)]
  transfers between devices with their start and end apart: 5 -> 14, of which waited for: 1 -> 7; matrix products, arithmetic and copies ran while one was open for 0% -> 0% of each run, Pallas kernels for 38% -> 41%
where the time goes in v2:
time: 121 us; the launch traced here: 120 us
  Pallas kernels  55.7 us (46%)
  waiting for transfers between devices  34 us (28%)
  starting transfers between devices  26 us (21%)
  local copies, waits for them, and re-layouts  2.92 us (2%)
  between operations  1.43 us (1%)
    ppermute x6, waiting for transfers between devices, shifted(): return lax.ppermute(block, axis, route)  26.3 us
    pallas_call x1, Pallas kernels, on_device(): pl.pallas_call(functools.partial(pairs_kernel, per_mol), grid=(pairs // B...  23.7 us
    pallas_call x1, Pallas kernels, on_device(): pl.pallas_call(functools.partial(turned_kernel, per_mol), grid=(pairs //...  21.3 us
    ppermute x7, starting transfers between devices, ahead(): return lax.ppermute(block, 'sub', route)  12.5 us
    ppermute x6, starting transfers between devices, shifted(): return lax.ppermute(block, axis, route)  8.59 us
    all_to_all x1, waiting for transfers between devices, on_device(): received = lax.all_to_all(payload, 'sub', 0, 0, tiled=True)  7.54 us
    all_to_all x1, starting transfers between devices, on_device(): received = lax.all_to_all(payload, 'sub', 0, 0, tiled=True)  4.87 us
    pallas_call x1, Pallas kernels, on_device(): pl.pallas_call(collect_kernel, grid=(teams // group,), out_shape=(shape((...  4.52 us
  transfers between devices with their start and end apart: 14, of which 7 were waited for; matrix products, arithmetic and copies ran while one was open for 0% of the time, Pallas kernels for 41%

profile of v2, /device:TPU:6, one launch (start us, length us, event | category | flops | bytes accessed | tf_op | source)
XLA Modules:
  0.0 120.3 jit_solution(9955350059478754256)
XLA Ops:
  0.6 1.1 copy-done.2
  2.5 1.9 %collective-permute-start.2 = (bf16[384,128]{1,0:T(8,128)(2,1)S(1)}, bf16[384,128]{1,0:T(8,128)(2,1)S(1)}, u32[]{:S(2)}, u32[]{:S(2)}) collective-permute-start(bf16[384,128]{1,0:T(8,128)(2,1)S(1)} %get-tuple-element.23), channel_id=1, source_target_pairs={{24,0},{25,1},{26,2},{27,3},{28,4},{29,5},{30,6},{31,7},{0,8},{1,9... | collective-permute-start | bytes 294920 | tf_op jit(solution)/shard_map/ppermute | solution.py:51
  4.5 3.6 %collective-permute-start.1 = (bf16[384,128]{1,0:T(8,128)(2,1)S(1)}, bf16[384,128]{1,0:T(8,128)(2,1)S(1)}, u32[]{:S(2)}, u32[]{:S(2)}) collective-permute-start(bf16[384,128]{1,0:T(8,128)(2,1)S(1)} %get-tuple-element.23), channel_id=1, source_target_pairs={{16,0},{17,1},{18,2},{19,3},{20,4},{21,5},{22,6},{23,7},{24,8},{25... | collective-permute-start | bytes 294920 | tf_op jit(solution)/shard_map/ppermute | solution.py:51
  8.0 1.0 collective-permute-start
  10.5 2.0 %rank.1 = (s32[24,128]{1,0:T(8,128)S(1)}, s32[24,128]{1,0:T(8,128)S(1)}, s32[24,128]{1,0:T(8,128)S(1)}, s32[24,128]{1,0:T(8,128)S(1)}, s32[128,128]{1,0:T(8,128)S(1)}, /*index=5*/f32[128,128]{1,0:T(8,128)S(1)}) custom-call(s32[4]{0:T(128)S(1)} %pad_add_fusion.info, s32[24,128]{1,0:T(8,128)S(1)} %bitcast.15), custom_call_target="tpu_custom_call" | custom-call | bytes 10800000 | tf_op jit(solution)/shard_map/rank/pallas_call | solution.py:397
  13.1 1.6 %collective-permute-start.5 = (bf16[4,384,128]{2,1,0:T(8,128)(2,1)S(1)}, bf16[4,384,128]{2,1,0:T(8,128)(2,1)S(1)}, u32[]{:S(2)}, u32[]{:S(2)}) collective-permute-start(bf16[4,384,128]{2,1,0:T(8,128)(2,1)S(1)} %pad_maximum_fusion.1), channel_id=1, source_target_pairs={{6,0},{7,1},{0,2},{1,3},{2,4},{3,5},{4,6},{5,7},{14,8},{15,9},{8,1... | collective-permute-start | bytes 1179656 | tf_op jit(solution)/shard_map/ppermute | solution.py:51
  14.7 2.9 %collective-permute-start.4 = (bf16[4,384,128]{2,1,0:T(8,128)(2,1)S(1)}, bf16[4,384,128]{2,1,0:T(8,128)(2,1)S(1)}, u32[]{:S(2)}, u32[]{:S(2)}) collective-permute-start(bf16[4,384,128]{2,1,0:T(8,128)(2,1)S(1)} %pad_maximum_fusion.1), channel_id=1, source_target_pairs={{4,0},{5,1},{6,2},{7,3},{0,4},{1,5},{2,6},{3,7},{12,8},{13,9},{14,... | collective-permute-start | bytes 1179656 | tf_op jit(solution)/shard_map/ppermute | solution.py:51
  17.6 1.3 %collective-permute-start.3 = (bf16[4,384,128]{2,1,0:T(8,128)(2,1)S(1)}, bf16[4,384,128]{2,1,0:T(8,128)(2,1)S(1)}, u32[]{:S(2)}, u32[]{:S(2)}) collective-permute-start(bf16[4,384,128]{2,1,0:T(8,128)(2,1)S(1)} %pad_maximum_fusion.1), channel_id=1, source_target_pairs={{2,0},{3,1},{4,2},{5,3},{6,4},{7,5},{0,6},{1,7},{10,8},{11,9},{12,... | collective-permute-start | bytes 1179656 | tf_op jit(solution)/shard_map/ppermute | solution.py:51
  19.0 21.3 %turned.1 = bf16[32,592,128]{2,1,0:T(8,128)(2,1)} custom-call(s32[3072]{0:T(1024)} %bitcast.14, s32[4]{0:T(128)} %copy-done.5, bf16[192,256]{1,0:T(8,128)(2,1)} %copy-done, bf16[1152,3072]{1,0:T(8,128)(2,1)} %blocks.5, f32[128,128]{1,0:T(8,128)} %copy-done.4), custom_call_target="tpu_custom_call" | custom-call | bytes 90000000 | tf_op jit(solution)/shard_map/turned/pallas_call | solution.py:413
  40.5 4.9 %all-to-all-start = ((bf16[32,592,128]{2,1,0:T(8,128)(2,1)}), bf16[32,592,128]{2,1,0:T(8,128)(2,1)}, u32[]{:S(2)}, u32[]{:S(2)}) async-start(bf16[32,592,128]{2,1,0:T(8,128)(2,1)} %turned.1), calls=%async_computation | async-start | bytes 9699328 | tf_op jit(solution)/shard_map/all_to_all | solution.py:439
  46.4 2.4 %collective-permute-start.7 = (s32[128,128]{1,0:T(8,128)S(1)}, s32[128,128]{1,0:T(8,128)S(1)}, u32[]{:S(2)}, u32[]{:S(2)}) collective-permute-start(s32[128,128]{1,0:T(8,128)S(1)} %get-tuple-element.34), channel_id=1, source_target_pairs={{96,0},{0,32},{32,64},{64,96},{97,1},{1,33},{33,65},{65,97},{98,2}... | collective-permute-start | bytes 196616 | tf_op jit(solution)/shard_map/ppermute | solution.py:365
  48.9 2.3 %collective-permute-done.8.from_upper = s32[128,128]{1,0:T(8,128)S(1)} collective-permute-done((s32[128,128]{1,0:T(8,128)S(1)}, s32[128,128]{1,0:T(8,128)S(1)}, u32[]{:S(2)}, u32[]{:S(2)}) %collective-permute-start.8) | collective-permute-done | bytes 65568 | tf_op jit(solution)/shard_map/ppermute | solution.py:365
  51.2 1.3 %answer.1 = (bf16[32,96,128]{2,1,0:T(8,128)(2,1)S(1)}, bf16[32,96,128]{2,1,0:T(8,128)(2,1)S(1)}) custom-call(s32[128,128]{1,0:T(8,128)S(1)} %collective-permute-done.7.from_lower, s32[128,128]{1,0:T(8,128)S(1)} %collective-permute-done.8.from_upper, bf16[16,384,128]{2,1,0:T(8,128)(2,1)S(1)} %pad_maximum_fusion.same, ...), custom_call_target="tpu_custom_call" | custom-call | tf_op jit(solution)/shard_map/answer/pallas_call | solution.py:442
  52.5 3.2 %collective-permute-start.9 = (bf16[32,96,128]{2,1,0:T(8,128)(2,1)S(1)}, bf16[32,96,128]{2,1,0:T(8,128)(2,1)S(1)}, u32[]{:S(2)}, u32[]{:S(2)}) collective-permute-start(bf16[32,96,128]{2,1,0:T(8,128)(2,1)S(1)} %get-tuple-element.35), channel_id=1, source_target_pairs={{96,0},{0,32},{32,64},{64,96},{97,1},{1,33},{33,65},{65,97},{98,2}... | collective-permute-start | bytes 2359304 | tf_op jit(solution)/shard_map/ppermute | solution.py:365
  55.7 1.0 diagonal.1.local
  56.7 15.3 %collective-permute-done.9.lower = bf16[32,96,128]{2,1,0:T(8,128)(2,1)S(1)} collective-permute-done((bf16[32,96,128]{2,1,0:T(8,128)(2,1)S(1)}, bf16[32,96,128]{2,1,0:T(8,128)(2,1)S(1)}, u32[]{:S(2)}, u32[]{:S(2)}) %collective-permute-start.9) | collective-permute-done | bytes 786464 | tf_op jit(solution)/shard_map/ppermute | solution.py:365
  72.0 3.4 %collective-permute-done.10.upper = bf16[32,96,128]{2,1,0:T(8,128)(2,1)S(1)} collective-permute-done((bf16[32,96,128]{2,1,0:T(8,128)(2,1)S(1)}, bf16[32,96,128]{2,1,0:T(8,128)(2,1)S(1)}, u32[]{:S(2)}, u32[]{:S(2)}) %collective-permute-start.10) | collective-permute-done | bytes 786464 | tf_op jit(solution)/shard_map/ppermute | solution.py:365
  75.4 23.7 %pairs.1 = (f32[128,3072]{1,0:T(8,128)}, f32[384,256]{1,0:T(8,128)S(1)}) custom-call(s32[3072]{0:T(1024)S(1)} %bitcast.12, s32[3072]{0:T(1024)S(1)} %bitcast.13, s32[4]{0:T(128)S(1)} %copy-done.6, bf16[192,256]{1,0:T(8,128)(2,1)S(1)} %copy-done.1, bf16[1152,3072]{1,0:T(8,128)(2,1)} %blocks.5, s32[24,128]{1,0:T(8,128)S(1)} %get-tuple-element.32.half, ...), custom_call_target="tpu_custom_call" | custom-call | bytes 126000000 | tf_op jit(solution)/shard_map/pairs/pallas_call | solution.py:470
  99.1 7.5 %all-to-all-done.blocks = bf16[32,592,128]{2,1,0:T(8,128)(2,1)} async-done(((bf16[32,592,128]{2,1,0:T(8,128)(2,1)}), bf16[32,592,128]{2,1,0:T(8,128)(2,1)}, u32[]{:S(2)}, u32[]{:S(2)}) %all-to-all-start) | async-done | bytes 4849696 | tf_op jit(solution)/shard_map/all_to_all | solution.py:439
  106.6 4.5 %collect.1 = (bf16[256,384]{1,0:T(8,128)(2,1)S(1)}, f32[256,384]{1,0:T(8,128)S(1)}, bf16[256,384]{1,0:T(8,128)(2,1)S(1)}) custom-call(bf16[32,592,128]{2,1,0:T(8,128)(2,1)} %all-to-all-done.blocks), custom_call_target="tpu_custom_call" | custom-call | tf_op jit(solution)/shard_map/collect/pallas_call | solution.py:508
  111.7 1.6 %collective-permute-start.12 = (bf16[256,384]{1,0:T(8,128)(2,1)S(1)}, bf16[256,384]{1,0:T(8,128)(2,1)S(1)}, u32[]{:S(2)}, u32[]{:S(2)}) collective-permute-start(bf16[256,384]{1,0:T(8,128)(2,1)S(1)} %get-tuple-element.42), channel_id=1, source_target_pairs={{32,0},{64,32},{96,64},{0,96},{33,1},{65,33},{97,65},{1,97},{34,2}... | collective-permute-start | bytes 589832 | tf_op jit(solution)/shard_map/ppermute | solution.py:365
  113.3 3.6 %collective-permute-done.11.from_lower = bf16[256,384]{1,0:T(8,128)(2,1)S(1)} collective-permute-done((bf16[256,384]{1,0:T(8,128)(2,1)S(1)}, bf16[256,384]{1,0:T(8,128)(2,1)S(1)}, u32[]{:S(2)}, u32[]{:S(2)}) %collective-permute-start.11) | collective-permute-done | bytes 196640 | tf_op jit(solution)/shard_map/ppermute | solution.py:365
  116.9 1.7 %collective-permute-done.12.from_upper = bf16[256,384]{1,0:T(8,128)(2,1)S(1)} collective-permute-done((bf16[256,384]{1,0:T(8,128)(2,1)S(1)}, bf16[256,384]{1,0:T(8,128)(2,1)S(1)}, u32[]{:S(2)}, u32[]{:S(2)}) %collective-permute-start.12) | collective-permute-done | bytes 196640 | tf_op jit(solution)/shard_map/ppermute | solution.py:365
  118.6 1.7 %finish.1 = f32[384,256]{1,0:T(8,128)} custom-call(s32[4]{0:T(128)S(1)} %copy-done.6, f32[384,256]{1,0:T(8,128)S(1)} %get-tuple-element.38.total, f32[256,384]{1,0:T(8,128)S(1)} %get-tuple-element.40.here, bf16[256,384]{1,0:T(8,128)(2,1)S(1)} %collective-permute-done.11.from_lower, bf16[256,384]{1,0:T(8,128)(2,1)S(1)} %collective-permute-done.12.from_upper), custom_call_target="tpu_custom_call" | custom-call | tf_op jit(solution)/shard_map/finish/pallas_call | solution.py:520
  (33 shorter events, 4.0 us)
Async XLA Ops:
  0.6 1.1 copy-start.2
  1.9 0.6 copy-start
  2.5 10.0 %collective-permute-start.2 = (bf16[384,128]{1,0:T(8,128)(2,1)S(1)}, bf16[384,128]{1,0:T(8,128)(2,1)S(1)}, u32[]{:S(2)}, u32[]{:S(2)}) collective-permute-start(bf16[384,128]{1,0:T(8,128)(2,1)S(1)} %get-tuple-element.23), channel_id=1, source_target_pairs={{24,0},{25,1},{26,2},{27,3},{28,4},{29,5},{30,6},{31,7},{0,8},{1,9... | collective-permute-start | bytes 294920 | tf_op jit(solution)/shard_map/ppermute | solution.py:51
  4.5 8.2 %collective-permute-start.1 = (bf16[384,128]{1,0:T(8,128)(2,1)S(1)}, bf16[384,128]{1,0:T(8,128)(2,1)S(1)}, u32[]{:S(2)}, u32[]{:S(2)}) collective-permute-start(bf16[384,128]{1,0:T(8,128)(2,1)S(1)} %get-tuple-element.23), channel_id=1, source_target_pairs={{16,0},{17,1},{18,2},{19,3},{20,4},{21,5},{22,6},{23,7},{24,8},{25... | collective-permute-start | bytes 294920 | tf_op jit(solution)/shard_map/ppermute | solution.py:51
  8.0 4.6 %collective-permute-start = (bf16[384,128]{1,0:T(8,128)(2,1)S(1)}, bf16[384,128]{1,0:T(8,128)(2,1)S(1)}, u32[]{:S(2)}, u32[]{:S(2)}) collective-permute-start(bf16[384,128]{1,0:T(8,128)(2,1)S(1)} %get-tuple-element.23), channel_id=1, source_target_pairs={{8,0},{9,1},{10,2},{11,3},{12,4},{13,5},{14,6},{15,7},{16,8},{17,9... | collective-permute-start | bytes 294920 | tf_op jit(solution)/shard_map/ppermute | solution.py:51
  9.8 9.2 %copy-start.5 = (s32[4]{0:T(128)}, s32[4]{0:T(128)S(1)}, u32[]{:S(2)}) copy-start(s32[4]{0:T(128)S(1)} %pad_add_fusion.info) | copy-start | bytes 52
  9.8 0.7 copy-start.8
  12.5 0.6 copy-start.4
  12.5 0.6 copy-start.7
  13.1 27.1 %collective-permute-start.5 = (bf16[4,384,128]{2,1,0:T(8,128)(2,1)S(1)}, bf16[4,384,128]{2,1,0:T(8,128)(2,1)S(1)}, u32[]{:S(2)}, u32[]{:S(2)}) collective-permute-start(bf16[4,384,128]{2,1,0:T(8,128)(2,1)S(1)} %pad_maximum_fusion.1), channel_id=1, source_target_pairs={{6,0},{7,1},{0,2},{1,3},{2,4},{3,5},{4,6},{5,7},{14,8},{15,9},{8,1... | collective-permute-start | bytes 1179656 | tf_op jit(solution)/shard_map/ppermute | solution.py:51
  14.7 25.6 %collective-permute-start.4 = (bf16[4,384,128]{2,1,0:T(8,128)(2,1)S(1)}, bf16[4,384,128]{2,1,0:T(8,128)(2,1)S(1)}, u32[]{:S(2)}, u32[]{:S(2)}) collective-permute-start(bf16[4,384,128]{2,1,0:T(8,128)(2,1)S(1)} %pad_maximum_fusion.1), channel_id=1, source_target_pairs={{4,0},{5,1},{6,2},{7,3},{0,4},{1,5},{2,6},{3,7},{12,8},{13,9},{14,... | collective-permute-start | bytes 1179656 | tf_op jit(solution)/shard_map/ppermute | solution.py:51
  17.6 22.7 %collective-permute-start.3 = (bf16[4,384,128]{2,1,0:T(8,128)(2,1)S(1)}, bf16[4,384,128]{2,1,0:T(8,128)(2,1)S(1)}, u32[]{:S(2)}, u32[]{:S(2)}) collective-permute-start(bf16[4,384,128]{2,1,0:T(8,128)(2,1)S(1)} %pad_maximum_fusion.1), channel_id=1, source_target_pairs={{2,0},{3,1},{4,2},{5,3},{6,4},{7,5},{0,6},{1,7},{10,8},{11,9},{12,... | collective-permute-start | bytes 1179656 | tf_op jit(solution)/shard_map/ppermute | solution.py:51
  40.5 66.1 %all-to-all-start = ((bf16[32,592,128]{2,1,0:T(8,128)(2,1)}), bf16[32,592,128]{2,1,0:T(8,128)(2,1)}, u32[]{:S(2)}, u32[]{:S(2)}) async-start(bf16[32,592,128]{2,1,0:T(8,128)(2,1)} %turned.1), calls=%async_computation | async-start | bytes 9699328 | tf_op jit(solution)/shard_map/all_to_all | solution.py:439
  45.4 5.8 %collective-permute-start.6 = (bf16[16,384,128]{2,1,0:T(8,128)(2,1)S(1)}, bf16[16,384,128]{2,1,0:T(8,128)(2,1)S(1)}, u32[]{:S(2)}, u32[]{:S(2)}) collective-permute-start(bf16[16,384,128]{2,1,0:T(8,128)(2,1)S(1)} %pad_maximum_fusion.same), channel_id=1, source_target_pairs={{1,0},{0,1},{3,2},{2,3},{5,4},{4,5},{7,6},{6,7},{9,8},{8,9},{11,10... | collective-permute-start | bytes 4718600 | tf_op jit(solution)/shard_map/ppermute | solution.py:51
  45.6 10.1 %copy-start.1 = (bf16[192,256]{1,0:T(8,128)(2,1)S(1)}, bf16[192,256]{1,0:T(8,128)(2,1)}, u32[]{:S(2)}) copy-start(bf16[192,256]{1,0:T(8,128)(2,1)} %copy-done) | copy-start | bytes 294916
  45.6 10.1 %copy-start.3 = (bf16[1152,256]{1,0:T(8,128)(2,1)S(1)}, bf16[1152,256]{1,0:T(8,128)(2,1)}, u32[]{:S(2)}) copy-start(bf16[1152,256]{1,0:T(8,128)(2,1)} %blocks.4) | copy-start | bytes 1769476
  45.6 29.8 %copy-start.6 = (s32[4]{0:T(128)S(1)}, s32[4]{0:T(128)}, u32[]{:S(2)}) copy-start(s32[4]{0:T(128)} %copy-done.5) | copy-start | bytes 52
  45.6 5.6 %collective-permute-start.8 = (s32[128,128]{1,0:T(8,128)S(1)}, s32[128,128]{1,0:T(8,128)S(1)}, u32[]{:S(2)}, u32[]{:S(2)}) collective-permute-start(s32[128,128]{1,0:T(8,128)S(1)} %get-tuple-element.34), channel_id=1, source_target_pairs={{32,0},{64,32},{96,64},{0,96},{33,1},{65,33},{97,65},{1,97},{34,2}... | collective-permute-start | bytes 196616 | tf_op jit(solution)/shard_map/ppermute | solution.py:365
  46.4 4.7 %collective-permute-start.7 = (s32[128,128]{1,0:T(8,128)S(1)}, s32[128,128]{1,0:T(8,128)S(1)}, u32[]{:S(2)}, u32[]{:S(2)}) collective-permute-start(s32[128,128]{1,0:T(8,128)S(1)} %get-tuple-element.34), channel_id=1, source_target_pairs={{96,0},{0,32},{32,64},{64,96},{97,1},{1,33},{33,65},{65,97},{98,2}... | collective-permute-start | bytes 196616 | tf_op jit(solution)/shard_map/ppermute | solution.py:365
  52.5 19.5 %collective-permute-start.9 = (bf16[32,96,128]{2,1,0:T(8,128)(2,1)S(1)}, bf16[32,96,128]{2,1,0:T(8,128)(2,1)S(1)}, u32[]{:S(2)}, u32[]{:S(2)}) collective-permute-start(bf16[32,96,128]{2,1,0:T(8,128)(2,1)S(1)} %get-tuple-element.35), channel_id=1, source_target_pairs={{96,0},{0,32},{32,64},{64,96},{97,1},{1,33},{33,65},{65,97},{98,2}... | collective-permute-start | bytes 2359304 | tf_op jit(solution)/shard_map/ppermute | solution.py:365
  55.7 19.7 %collective-permute-start.10 = (bf16[32,96,128]{2,1,0:T(8,128)(2,1)S(1)}, bf16[32,96,128]{2,1,0:T(8,128)(2,1)S(1)}, u32[]{:S(2)}, u32[]{:S(2)}) collective-permute-start(bf16[32,96,128]{2,1,0:T(8,128)(2,1)S(1)} %get-tuple-element.36), channel_id=1, source_target_pairs={{32,0},{64,32},{96,64},{0,96},{33,1},{65,33},{97,65},{1,97},{34,2}... | collective-permute-start | bytes 2359304 | tf_op jit(solution)/shard_map/ppermute | solution.py:365
  111.2 5.7 %collective-permute-start.11 = (bf16[256,384]{1,0:T(8,128)(2,1)S(1)}, bf16[256,384]{1,0:T(8,128)(2,1)S(1)}, u32[]{:S(2)}, u32[]{:S(2)}) collective-permute-start(bf16[256,384]{1,0:T(8,128)(2,1)S(1)} %get-tuple-element.41), channel_id=1, source_target_pairs={{96,0},{0,32},{32,64},{64,96},{97,1},{1,33},{33,65},{65,97},{98,2}... | collective-permute-start | bytes 589832 | tf_op jit(solution)/shard_map/ppermute | solution.py:365
  111.7 6.9 %collective-permute-start.12 = (bf16[256,384]{1,0:T(8,128)(2,1)S(1)}, bf16[256,384]{1,0:T(8,128)(2,1)S(1)}, u32[]{:S(2)}, u32[]{:S(2)}) collective-permute-start(bf16[256,384]{1,0:T(8,128)(2,1)S(1)} %get-tuple-element.42), channel_id=1, source_target_pairs={{32,0},{64,32},{96,64},{0,96},{33,1},{65,33},{97,65},{1,97},{34,2}... | collective-permute-start | bytes 589832 | tf_op jit(solution)/shard_map/ppermute | solution.py:365

commit v3 on v2

--- a/solution.py
+++ b/solution.py
@@ -14,9 +14,12 @@
 CAP = 64
 LANES = 128
 BLOCK = 4 * LANES
-BATCH = 64
+MOVES = 16
 SIDES = 3
-RING = 4
+CHIPS = 16
+MAIN = 160
+SPARE = SIDES * CAP - MAIN
+TAILS = LANES // SPARE
 KEYS = 4
 ASPC_WEIGHTS = (2.8, -2.8, 1.2, -0.2)
 VMEM = pl.BlockSpec(memory_space=pltpu.VMEM)
@@ -31,24 +34,11 @@
 
 
 def relative(team, me):
-    z = (team // (2 * RING) - me // (2 * RING) + RING) % RING
-    y = (team // 2 % RING - me // 2 % RING + RING) % RING
-    return (team % 2 + me) % 2 * RING * RING + y * RING + z
+    return (team + me) % 2 * CHIPS + team // 2
 
 
 def absolute(place, me):
-    z = (place + me // (2 * RING)) % RING
-    y = (place // RING + me // 2) % RING
-    return (z * RING + y) * 2 + (place // (RING * RING) + me) % 2
-
-
-def ahead(block, dz, dy, core):
-    route = []
-    for target in range(2 * RING * RING):
-        z, y, c = target // (2 * RING), target // 2 % RING, target % 2
-        source = ((z + dz) % RING * RING + (y + dy) % RING) * 2 + (c + core) % 2
-        route.append((source, target))
-    return lax.ppermute(block, "sub", route)
+    return place % CHIPS * 2 + (place // CHIPS + me) % 2
 
 
 def predict_kernel(history, guess, rows):
@@ -59,24 +49,25 @@
     rounded = total.astype(jnp.bfloat16)
     guess[...] = rounded
     wide = rounded.astype(jnp.float32)
+    packed = []
     for part in range(mols // LANES):
-        cut = slice(part * LANES, (part + 1) * LANES)
-        rows[cut, :] = wide[:LANES, cut].T.astype(jnp.bfloat16)
-    rest = jnp.concatenate([wide[LANES:, :LANES], wide[LANES:, LANES:]], axis=0)
-    rows[mols:, :] = rest.T.astype(jnp.bfloat16)
+        packed.append(wide[:LANES, part * LANES : (part + 1) * LANES].T)
+    packed.append(jnp.concatenate([wide[LANES:, :LANES], wide[LANES:, LANES:]], axis=0).T)
+    packed = jnp.concatenate(packed, axis=0).astype(jnp.bfloat16)
+    for chip in range(rows.shape[0]):
+        rows[chip] = packed
 
 
 def rank_kernel(
-    teams, domains, mols, info, near, dest, first_rows, rest_rows, half, wanted, label
+    teams, domains, mols, info, near, dest, first_rows, rest_rows, half, wanted, label,
+    ones, sums, named, ranks, known, spots,
 ):
     my_domain = info[0]
-    parity = info[2]
     listed = near[...]
     owner = listed // mols
     slot = listed % mols
     team = relative(owner % teams, info[3])
     offset = (owner // teams - my_domain + 1 + domains) % domains
-    place = team * WIDTH + offset * CAP
     inside = offset == 1
     held_rows = mols * FEAT // LANES
     beyond = teams * held_rows + (offset // 2 * teams + team) * PACKED
@@ -85,17 +76,30 @@
     square = (LANES, 2 * LANES)
     before = ((iota(square, 0) < iota(square, 1)) | (iota(square, 1) >= LANES)).astype(jnp.bfloat16)
     which = iota((keys, LANES), 0)
-    carry = jnp.zeros((keys, LANES), jnp.float32)
-    names = jnp.zeros((keys, LANES), jnp.float32)
-    for block in range(listed.shape[0]):
+    who = iota((teams, LANES), 0)
+    count = keys + teams
+    blocks = listed.shape[0]
+    for block in range(blocks):
         at = slice(block, block + 1)
+        both = [jnp.where(which == key[at], 1.0, 0.0), jnp.where(who == team[at], 1.0, 0.0)]
+        ones[block * count : (block + 1) * count, :] = jnp.concatenate(both, axis=0).astype(
+            jnp.bfloat16
+        )
+    sums[...] = jnp.dot(ones[...], before, preferred_element_type=jnp.float32)
+    carry = jnp.zeros((count, LANES), jnp.float32)
+    last = jnp.zeros((1, LANES), jnp.int32)
+    for block in range(blocks):
+        at = slice(block, block + 1)
+        cut = slice(block * LANES, (block + 1) * LANES)
         hit = which == key[at]
-        ones = jnp.where(hit, 1.0, 0.0)
-        sums = jnp.dot(ones.astype(jnp.bfloat16), before, preferred_element_type=jnp.float32)
-        prior = sums[:, :LANES] + carry
-        carry = carry + sums[:, LANES:]
-        rank = jnp.sum(jnp.where(hit, prior, 0.0), axis=0, keepdims=True).astype(jnp.int32)
-        dest[at, :] = place[at] + rank
+        peer = who == team[at]
+        first = block * count
+        prior = sums[first : first + count, :LANES] + carry
+        carry = carry + sums[first : first + count, LANES:]
+        rank = jnp.sum(jnp.where(hit, prior[:keys], 0.0), axis=0, keepdims=True).astype(jnp.int32)
+        spot = jnp.sum(jnp.where(peer, prior[keys:], 0.0), axis=0, keepdims=True).astype(jnp.int32)
+        last = jnp.maximum(last, spot)
+        dest[at, :] = team[at] * WIDTH + spot
         base = team[at] * held_rows
         first_rows[at, :] = jnp.where(inside[at], base + slot[at], beyond[at] + rank)
         rest_rows[at, :] = jnp.where(
@@ -104,16 +108,25 @@
             beyond[at] + CAP + rank % (CAP // 2),
         )
         half[at, :] = jnp.where(inside[at], slot[at] // LANES, rank // (CAP // 2))
-        column = iota((LANES, LANES), 0) == rank
-        named = jnp.where(hit, slot[at].astype(jnp.float32), 0.0)
-        names = names + lax.dot_general(
-            named.astype(jnp.bfloat16),
-            column.astype(jnp.bfloat16),
-            NT,
-            preferred_element_type=jnp.float32,
-        )
+        name = slot[at].astype(jnp.float32)
+        named[:, cut] = jnp.where(hit, name, 0.0).astype(jnp.bfloat16)
+        ranks[:, cut] = (iota((LANES, LANES), 0) == rank).astype(jnp.bfloat16)
+        side = offset[at].astype(jnp.float32)
+        both = [jnp.where(peer, name, 0.0), jnp.where(peer, side, 0.0)]
+        known[:, cut] = jnp.concatenate(both, axis=0).astype(jnp.bfloat16)
+        spots[:, cut] = (iota((2 * LANES, LANES), 0) == spot).astype(jnp.bfloat16)
+    names = lax.dot_general(named[...], ranks[...], NT, preferred_element_type=jnp.float32)
+    filed = lax.dot_general(known[...], spots[...], NT, preferred_element_type=jnp.float32)
     wanted[...] = names.astype(jnp.int32)
-    label[...] = jnp.where(parity == 1, pltpu.roll(names, CAP, 1), names)
+    shift = info[3] % TAILS * SPARE
+    back = (shift + LANES - SPARE) % LANES
+    for at in range(2):
+        part = filed[at * teams : (at + 1) * teams]
+        label[2 * at] = part[:, :LANES]
+        label[2 * at + 1] = pltpu.roll(part[:, LANES:], shift, 1)
+        label[5 + at] = pltpu.roll(part[:, LANES:], back, 1)
+    over = jnp.max(last, axis=1, keepdims=True) >= MAIN
+    label[4] = jnp.broadcast_to(jnp.where(over, 1.0, 0.0), (teams, LANES))
 
 
 def answer_kernel(from_lower, from_upper, same, other, to_lower, to_upper):
@@ -151,13 +164,15 @@
     return (iota((mols, BLOCK), 0) == mol).astype(jnp.bfloat16)
 
 
-def turned_kernel(per_mol, dest, info, guess, blocks, label, out, wide, mine, turned, slots, stage, sems):
+def turned_kernel(per_mol, dest, info, guess, blocks, label, out, spare, mine, turned, slots, stage, rest, sems):
     step = pl.program_id(0)
     teams = out.shape[0]
     width = WIDTH
 
     @pl.when(step == 0)
     def _():
+        turned[...] = jnp.zeros_like(turned)
+
         def clear(team, _):
             start = pl.multiple_of(team * width, width)
             for part in range(3):
@@ -169,15 +184,28 @@
     table = owners(guess.shape[1], step * BLOCK, per_mol, info[1])
     mine[...] = jnp.dot(guess[...], table, preferred_element_type=jnp.float32)
 
+    def move(line):
+        for first in range(0, LANES, MOVES):
+            places = [dest[line + first + i] for i in range(MOVES)]
+            rows = [
+                [turned[part, first + i : first + i + 1, :] for part in range(3)]
+                for i in range(MOVES)
+            ]
+            for place, row in zip(places, rows):
+                for part in range(3):
+                    slots[part, pl.ds(place, 1), :] = row[part]
+
     def column(at, _):
         cut = pl.ds(pl.multiple_of(at * LANES, LANES), LANES)
-        wide[...] = blocks[:, cut].astype(jnp.float32)
+        move(jnp.maximum(step * BLOCK + (at - 1) * LANES, 0))
         results = []
         for side in range(2):
             sums = [[None] * 3 for _ in range(OCC)]
             for inner in range(BAS):
                 first = (side * BAS + inner) * BAS
-                block = [wide[first + 8 * g : first + 8 * g + 8, :] for g in range(3)]
+                block = [
+                    blocks[first + 8 * g : first + 8 * g + 8, cut].astype(jnp.float32) for g in range(3)
+                ]
                 for k in range(OCC):
                     row = mine[inner * OCC + k : inner * OCC + k + 1, cut]
                     for g in range(3):
@@ -187,45 +215,45 @@
         for part in range(3):
             turned[part] = jnp.concatenate(results[part * 16 : part * 16 + 16], axis=0).T
 
-        line = step * BLOCK + at * LANES
-
-        def move(first, _):
-            first = pl.multiple_of(first * BATCH, BATCH)
-            places = [dest[line + first + i] for i in range(BATCH)]
-            rows = [
-                [turned[part, pl.ds(first + i, 1), :] for part in range(3)] for i in range(BATCH)
-            ]
-            for place, row in zip(places, rows):
-                for part in range(3):
-                    slots[part, pl.ds(place, 1), :] = row[part]
-            return 0
-
-        return lax.fori_loop(0, LANES // BATCH, move, 0)
+        return 0
 
     lax.fori_loop(0, BLOCK // LANES, column, 0)
 
     @pl.when(step == pl.num_programs(0) - 1)
     def _():
-        def copy(team):
-            return pltpu.make_async_copy(
-                stage.at[team], out.at[absolute(team, info[3])], sems.at[team]
-            )
+        move((step + 1) * BLOCK - LANES)
+
+        def copies(team):
+            peer = absolute(team, info[3])
+            return [
+                pltpu.make_async_copy(stage.at[team], out.at[peer], sems.at[0, team]),
+                pltpu.make_async_copy(rest.at[team], spare.at[peer], sems.at[1, team]),
+            ]
 
         def finish(team, _):
             start = pl.multiple_of(team * width, width)
             for part in range(3):
-                stage[team, part * width : (part + 1) * width, :] = slots[
-                    part, pl.ds(start, width), :
+                stage[team, part * MAIN : (part + 1) * MAIN, :] = slots[
+                    part, pl.ds(start, MAIN), :
                 ].astype(jnp.bfloat16)
-            names = label[pl.ds(pl.multiple_of(team // 2 * 8, 8), 8), :]
-            names = jnp.where(team % 2 == 1, pltpu.roll(names, KEYS, 0), names)
-            names = jnp.concatenate([names, jnp.zeros_like(names)], axis=0)
-            stage[team, 3 * width :, :] = names.astype(jnp.bfloat16)
-            copy(team).start()
+                rest[team, part * SPARE : (part + 1) * SPARE, :] = slots[
+                    part, pl.ds(start + MAIN, SPARE), :
+                ].astype(jnp.bfloat16)
+            names = [label[row, pl.ds(team, 1), :] for row in range(7)]
+            fill = jnp.zeros((16, LANES), jnp.float32)
+            stage[team, 3 * MAIN :, :] = jnp.concatenate(names[:5] + [fill[5:]], axis=0).astype(
+                jnp.bfloat16
+            )
+            rest[team, 3 * SPARE :, :] = jnp.concatenate(names[5:] + [fill[2:]], axis=0).astype(
+                jnp.bfloat16
+            )
+            for copy in copies(team):
+                copy.start()
             return 0
 
         def wait(team, _):
-            copy(team).wait()
+            for copy in copies(team):
+                copy.wait()
             return 0
 
         lax.fori_loop(0, teams, finish, 0)
@@ -283,24 +311,26 @@
     table = owners(mols, step * BLOCK, per_mol, info[1])
     mine[...] = jnp.dot(guess[...], table, preferred_element_type=jnp.float32)
 
+    def pick(line):
+        for first in range(0, LANES, MOVES):
+            for index, near in ((first_rows, near_a), (rest_rows, near_b)):
+                places = [index[line * LANES + first + i] for i in range(MOVES)]
+                rows = [held[pl.ds(place, 1), :] for place in places]
+                near[first : first + MOVES, :] = jnp.concatenate(rows, axis=0)
+
+    @pl.when(step == 0)
+    def _():
+        pick(0)
+
     def column(at, _):
         cut = pl.ds(pl.multiple_of(at * LANES, LANES), LANES)
         line = step * (BLOCK // LANES) + at
-
-        def pick(first, _):
-            first = pl.multiple_of(first * BATCH, BATCH)
-            for index, near in ((first_rows, near_a), (rest_rows, near_b)):
-                places = [index[line * LANES + first + i] for i in range(BATCH)]
-                rows = [held[pl.ds(place, 1), :] for place in places]
-                near[pl.ds(first, BATCH), :] = jnp.concatenate(rows, axis=0)
-            return 0
-
-        lax.fori_loop(0, LANES // BATCH, pick, 0)
         theirs[:LANES, :] = near_a[...].T
         rest = near_b[...].T
         theirs[LANES:, :] = jnp.where(
             half[pl.ds(line, 1), :] > 0, rest[FEAT - LANES :], rest[: FEAT - LANES]
         )
+        pick(jnp.minimum(line + 1, half.shape[0] - 1))
         wide[...] = blocks[:, cut].astype(jnp.float32)
         reduced = apply_blocks(wide, theirs, applied, mine, cut)
         scores[:, cut] = jnp.concatenate(reduced[0] + reduced[1], axis=0)
@@ -312,36 +342,77 @@
     )
 
 
-def collect_kernel(blocks, lower, here, upper, sums):
+def tail_names(labels, low, high, mols):
+    lane = iota((1, LANES), 1) // SPARE
+    names = jnp.zeros((1, LANES), jnp.float32)
+    for at, label in enumerate(labels):
+        name = label[low : low + 1] + label[high : high + 1] * mols
+        names = jnp.where(lane == at, name, names)
+    return names
+
+
+def collect_kernel(blocks, lower, here, upper, over, sums, flags):
     step = pl.program_id(0)
     mols = here.shape[0]
-    group = blocks.shape[0]
 
     @pl.when(step == 0)
     def _():
         sums[...] = jnp.zeros_like(sums)
-
-    mol = iota((mols, group * CAP), 0).astype(jnp.float32)
-    first = iota((1, LANES), 1) < CAP
-    labels = [blocks[i, 3 * WIDTH :, :].astype(jnp.float32) for i in range(group)]
-    for side in range(SIDES):
-        at = slice(side, side + 1)
-        names = [jnp.where(first, labels[i][at], labels[i + 1][at]) for i in range(0, group, 2)]
-        hit = (mol == jnp.concatenate(names, axis=1)).astype(jnp.bfloat16)
-        values = []
-        for part in range(3):
-            row = part * WIDTH + side * CAP
-            values.append(
-                jnp.concatenate([blocks[i, row : row + CAP, :] for i in range(group)], axis=0)
-            )
-        sums[side] += jnp.dot(
-            hit, jnp.concatenate(values, axis=1), preferred_element_type=jnp.float32
-        )
+        flags[...] = jnp.zeros_like(flags)
+
+    peers = range(blocks.shape[0])
+    labels = [blocks[i, 3 * MAIN :, :].astype(jnp.float32) for i in peers]
+    names = [label[0:1] + label[2:3] * mols for label in labels]
+    for first in range(0, len(labels), TAILS):
+        names.append(tail_names(labels[first : first + TAILS], 1, 3, mols))
+    names = jnp.concatenate(names, axis=1)
+    mol = iota((SIDES * mols, names.shape[1]), 0).astype(jnp.float32)
+    values = []
+    for part in range(3):
+        row = part * MAIN
+        rows = [blocks[i, row : row + LANES, :] for i in peers]
+        rows += [blocks[i, row + LANES : row + MAIN, :] for i in peers]
+        values.append(jnp.concatenate(rows, axis=0))
+    sums[...] += jnp.dot(
+        (mol == names).astype(jnp.bfloat16),
+        jnp.concatenate(values, axis=1),
+        preferred_element_type=jnp.float32,
+    )
+    for label in labels:
+        flags[...] = jnp.maximum(flags[...], label[:8])
 
     @pl.when(step == pl.num_programs(0) - 1)
     def _():
         for side, out in enumerate((lower, here, upper)):
-            out[...] = sums[side].astype(out.dtype)
+            out[...] = sums[side * mols : (side + 1) * mols].astype(out.dtype)
+        over[0] = (jnp.max(flags[4:5, :]) > 0).astype(jnp.int32)
+
+
+def spare_kernel(blocks, lower, here, upper, lower_out, here_out, upper_out):
+    mols = here.shape[0]
+    teams = blocks.shape[0]
+    names = []
+    for first in range(0, teams, TAILS):
+        labels = [
+            blocks[i, 3 * SPARE :, :].astype(jnp.float32) for i in range(first, first + TAILS)
+        ]
+        names.append(tail_names(labels, 0, 1, mols))
+    mol = iota((SIDES * mols, teams * SPARE), 0).astype(jnp.float32)
+    values = []
+    for part in range(3):
+        row = part * SPARE
+        values.append(
+            jnp.concatenate([blocks[i, row : row + SPARE, :] for i in range(teams)], axis=0)
+        )
+    sums = jnp.dot(
+        (mol == jnp.concatenate(names, axis=1)).astype(jnp.bfloat16),
+        jnp.concatenate(values, axis=1),
+        preferred_element_type=jnp.float32,
+    )
+    pairs = ((lower, lower_out), (here, here_out), (upper, upper_out))
+    for side, (before, out) in enumerate(pairs):
+        part = sums[side * mols : (side + 1) * mols]
+        out[...] = (before[...].astype(jnp.float32) + part).astype(out.dtype)
 
 
 def finish_kernel(info, total, here, from_lower, from_upper, out):
@@ -386,7 +457,7 @@
     info = jnp.stack([lax.axis_index("dom"), counts[0], lax.axis_index("sub") % 2, lax.axis_index("sub")]).astype(i32)
     guess, rows = pl.pallas_call(
         predict_kernel,
-        out_shape=(shape((FEAT, mols), bf16), shape((held_rows, LANES), bf16)),
+        out_shape=(shape((FEAT, mols), bf16), shape((CHIPS, held_rows, LANES), bf16)),
         in_specs=[VMEM],
         out_specs=(VMEM,) * 2,
         compiler_params=params(),
@@ -396,49 +467,61 @@
     table = shape((columns, LANES), i32)
     dest, first_rows, rest_rows, half, wanted, label = pl.pallas_call(
         functools.partial(rank_kernel, teams, domains, mols),
-        out_shape=(table,) * 4 + (shape((teams * KEYS, LANES), i32), shape((teams * KEYS, LANES), f32)),
+        out_shape=(table,) * 4 + (shape((teams * KEYS, LANES), i32), shape((7, teams, LANES), f32)),
         in_specs=[SMEM, VMEM],
         out_specs=(VMEM,) * 6,
+        scratch_shapes=[
+            pltpu.VMEM((columns * teams * (KEYS + 1), LANES), bf16),
+            pltpu.VMEM((columns * teams * (KEYS + 1), 2 * LANES), f32),
+            pltpu.VMEM((teams * KEYS, pairs), bf16),
+            pltpu.VMEM((LANES, pairs), bf16),
+            pltpu.VMEM((2 * teams, pairs), bf16),
+            pltpu.VMEM((2 * LANES, pairs), bf16),
+        ],
         compiler_params=params(),
         cost_estimate=cost(3),
         name="rank",
     )(info, neighbours.reshape(columns, LANES))
     dest, first_rows, rest_rows = (x.reshape(pairs) for x in (dest, first_rows, rest_rows))
 
-    same = jnp.stack([rows] + [ahead(rows, z, 0, 0) for z in range(1, RING)])
-    same, dest = lax.optimization_barrier((same, dest))
-    same = jnp.concatenate([same] + [ahead(same, 0, y, 0) for y in range(1, RING)])
+    cores = [[2 * chip + core for chip in range(CHIPS)] for core in range(2)]
+    same = lax.all_to_all(rows, "sub", 0, 0, tiled=True, axis_index_groups=cores)
     asked_lower, asked_upper = shifted(wanted, "dom", 1), shifted(wanted, "dom", -1)
 
-    payload = pl.pallas_call(
+    payload, spare = pl.pallas_call(
         functools.partial(turned_kernel, per_mol),
         grid=(pairs // BLOCK,),
-        out_shape=shape((teams, 3 * WIDTH + 16, LANES), bf16),
+        out_shape=(
+            shape((teams, 3 * MAIN + 16, LANES), bf16),
+            shape((teams, 3 * SPARE + 16, LANES), bf16),
+        ),
         in_specs=[
             SMEM,
             SMEM,
             pl.BlockSpec((FEAT, mols), lambda i: (0, 0)),
             pl.BlockSpec((6 * FEAT, BLOCK), lambda i: (0, i)),
-            pl.BlockSpec((teams * KEYS, LANES), lambda i: (0, 0)),
+            pl.BlockSpec((7, teams, LANES), lambda i: (0, 0, 0)),
         ],
-        out_specs=pl.BlockSpec(memory_space=pltpu.HBM),
+        out_specs=(pl.BlockSpec(memory_space=pltpu.HBM),) * 2,
         scratch_shapes=[
-            pltpu.VMEM((6 * FEAT, LANES), f32),
             pltpu.VMEM((FEAT, BLOCK), f32),
             pltpu.VMEM((3, LANES, LANES), f32),
             pltpu.VMEM((3, teams * WIDTH, LANES), f32),
-            pltpu.VMEM((teams, 3 * WIDTH + 16, LANES), bf16),
-            pltpu.SemaphoreType.DMA((teams,)),
+            pltpu.VMEM((teams, 3 * MAIN + 16, LANES), bf16),
+            pltpu.VMEM((teams, 3 * SPARE + 16, LANES), bf16),
+            pltpu.SemaphoreType.DMA((2, teams)),
         ],
         compiler_params=params(60),
         cost_estimate=cost(25),
         name="turned",
     )(dest, info, guess, pair_blocks, label)
 
-    payload, same = lax.optimization_barrier((payload, same))
+    payload, same, asked_lower, asked_upper = lax.optimization_barrier(
+        (payload, same, asked_lower, asked_upper)
+    )
     received = lax.all_to_all(payload, "sub", 0, 0, tiled=True)
 
-    other = ahead(same, 0, 0, 1)
+    other = lax.ppermute(same, "sub", [(i ^ 1, i) for i in range(teams)])
     to_lower, to_upper = pl.pallas_call(
         answer_kernel,
         out_shape=(shape((teams, PACKED, LANES), bf16),) * 2,
@@ -505,16 +588,32 @@
     received, total = lax.optimization_barrier((received, total))
     whole = pl.BlockSpec((mols, ROWS), lambda i: (0, 0))
     group = 8
-    below, here, above = pl.pallas_call(
+    sums_shape = (shape((mols, ROWS), bf16), shape((mols, ROWS), f32), shape((mols, ROWS), bf16))
+    below, here, above, over = pl.pallas_call(
         collect_kernel,
         grid=(teams // group,),
-        out_shape=(shape((mols, ROWS), bf16), shape((mols, ROWS), f32), shape((mols, ROWS), bf16)),
-        in_specs=[pl.BlockSpec((group, 3 * WIDTH + 16, LANES), lambda i: (i, 0, 0))],
-        out_specs=(whole,) * 3,
-        scratch_shapes=[pltpu.VMEM((SIDES, mols, ROWS), f32)],
+        out_shape=sums_shape + (shape((1,), i32),),
+        in_specs=[pl.BlockSpec((group, 3 * MAIN + 16, LANES), lambda i: (i, 0, 0))],
+        out_specs=(whole,) * 3 + (SMEM,),
+        scratch_shapes=[pltpu.VMEM((SIDES * mols, ROWS), f32), pltpu.VMEM((8, LANES), f32)],
         compiler_params=params(),
         name="collect",
     )(received)
+
+    def second_round(spare, *sums):
+        rest = lax.all_to_all(spare, "sub", 0, 0, tiled=True)
+        return pl.pallas_call(
+            spare_kernel,
+            out_shape=sums_shape,
+            in_specs=[VMEM] * 4,
+            out_specs=(VMEM,) * 3,
+            compiler_params=params(),
+            name="spare",
+        )(rest, *sums)
+
+    below, here, above = lax.cond(
+        over[0] > 0, second_round, lambda spare, *sums: sums, spare, below, here, above
+    )
     from_lower, from_upper = shifted(above, "dom", 1), shifted(below, "dom", -1)
 
     products = pl.pallas_call(

time: 121 us -> 117 us (0.967)
  waiting for transfers between devices: 34 us -> 28.8 us
  Pallas kernels: 55.7 us -> 58.8 us
  starting transfers between devices: 26 us -> 23.5 us
    ppermute x7 -> x1, starting transfers between devices: 12.5 us -> 0.29 us  [on_device(): other = lax.ppermute(same, 'sub', [(i ^ 1, i) for i in range(teams)])]
    all_to_all x0 -> x1, starting transfers between devices: none -> 8.18 us  [on_device(): lax.all_to_all(rows, 'sub', 0, 0, tiled=True, axis_index_groups=cores)]
    all_to_all x1, waiting for transfers between devices: 7.54 us -> 2.72 us  [on_device(): received = lax.all_to_all(payload, 'sub', 0, 0, tiled=True)]
    ppermute x6, waiting for transfers between devices: 26.3 us -> 22.9 us  [shifted(): return lax.ppermute(block, axis, route)]
    ppermute x7 -> x1, waiting for transfers between devices: 0.13 us -> 3.2 us  [on_device(): other = lax.ppermute(same, 'sub', [(i ^ 1, i) for i in range(teams)])]
    all_to_all x1, starting transfers between devices: 4.87 us -> 7.61 us  [on_device(): received = lax.all_to_all(payload, 'sub', 0, 0, tiled=True)]
    pallas_call x1, Pallas kernels: 4.52 us -> 6.86 us  [on_device(): pl.pallas_call(collect_kernel, grid=(teams // group,), out_shape=sums_sha...]
    pallas_call x1, Pallas kernels: 21.3 us -> 19.9 us  [on_device(): pl.pallas_call(functools.partial(turned_kernel, per_mol), grid=(pairs //...]
  transfers between devices with their start and end apart: 14 -> 9, of which waited for: 7 -> 6; matrix products, arithmetic and copies ran while one was open for 0% -> 0% of each run, Pallas kernels for 41% -> 42%
where the time goes in v3:
time: 117 us; the launch traced here: 116 us
  Pallas kernels  58.8 us (50%)
  waiting for transfers between devices  28.8 us (25%)
  starting transfers between devices  23.5 us (20%)
  local copies, waits for them, and re-layouts  3.02 us (3%)
  between operations  2.08 us (2%)
    pallas_call x1, Pallas kernels, on_device(): pl.pallas_call(functools.partial(pairs_kernel, per_mol), grid=(pairs // B...  23.5 us
    ppermute x6, waiting for transfers between devices, shifted(): return lax.ppermute(block, axis, route)  22.9 us
    pallas_call x1, Pallas kernels, on_device(): pl.pallas_call(functools.partial(turned_kernel, per_mol), grid=(pairs //...  19.9 us
    all_to_all x1, starting transfers between devices, on_device(): lax.all_to_all(rows, 'sub', 0, 0, tiled=True, axis_index_groups=cores)  8.18 us
    all_to_all x1, starting transfers between devices, on_device(): received = lax.all_to_all(payload, 'sub', 0, 0, tiled=True)  7.61 us
    ppermute x6, starting transfers between devices, shifted(): return lax.ppermute(block, axis, route)  7.43 us
    pallas_call x1, Pallas kernels, on_device(): pl.pallas_call(collect_kernel, grid=(teams // group,), out_shape=sums_sha...  6.86 us
    ppermute x1, waiting for transfers between devices, on_device(): other = lax.ppermute(same, 'sub', [(i ^ 1, i) for i in range(teams)])  3.2 us
  transfers between devices with their start and end apart: 9, of which 6 were waited for; matrix products, arithmetic and copies ran while one was open for 0% of the time, Pallas kernels for 42%

profile of v3, /device:TPU:6, one launch (start us, length us, event | category | flops | bytes accessed | tf_op | source)
XLA Modules:
  0.0 116.3 jit_solution(10920798702027609386)
XLA Ops:
  0.6 1.1 copy-done.2
  1.8 1.4 %predict.1 = (bf16[192,256]{1,0:T(8,128)(2,1)S(1)}, bf16[16,384,128]{2,1,0:T(8,128)(2,1)}) custom-call(f32[4,192,256]{2,1,0:T(8,128)S(1)} %copy-done.2), custom_call_target="tpu_custom_call" | custom-call | tf_op jit(solution)/shard_map/predict/pallas_call | solution.py:458
  3.2 0.6 copy-done
  3.8 8.2 %all-to-all-start.1 = ((bf16[16,384,128]{2,1,0:T(8,128)(2,1)}), bf16[16,384,128]{2,1,0:T(8,128)(2,1)S(1)}, u32[]{:S(2)}, u32[]{:S(2)}) async-start(bf16[16,384,128]{2,1,0:T(8,128)(2,1)} %get-tuple-element.51), calls=%async_computation.1 | async-start | bytes 3145728 | tf_op jit(solution)/shard_map/all_to_all | solution.py:488
  12.7 3.2 %rank.1 = (s32[24,128]{1,0:T(8,128)S(1)}, s32[24,128]{1,0:T(8,128)S(1)}, s32[24,128]{1,0:T(8,128)S(1)}, s32[24,128]{1,0:T(8,128)S(1)}, s32[128,128]{1,0:T(8,128)S(1)}, /*index=5*/f32[7,32,128]{2,1,0:T(8,128)S(1)}) custom-call(s32[4]{0:T(128)S(1)} %pad_add_fusion.info, s32[24,128]{1,0:T(8,128)S(1)} %bitcast.11), custom_call_target="tpu_custom_call" | custom-call | bytes 10800000 | tf_op jit(solution)/shard_map/rank/pallas_call | solution.py:468
  15.9 0.6 copy-done.4
  16.6 0.6 copy-done.7
  17.2 0.8 collective-permute-start.1
  18.0 2.4 %collective-permute-start = (s32[128,128]{1,0:T(8,128)S(1)}, s32[128,128]{1,0:T(8,128)S(1)}, u32[]{:S(2)}, u32[]{:S(2)}) collective-permute-start(s32[128,128]{1,0:T(8,128)S(1)} %get-tuple-element.52), channel_id=1, source_target_pairs={{96,0},{0,32},{32,64},{64,96},{97,1},{1,33},{33,65},{65,97},{98,2}... | collective-permute-start | bytes 196616 | tf_op jit(solution)/shard_map/ppermute | solution.py:436
  20.4 19.9 %turned.1 = (bf16[32,496,128]{2,1,0:T(8,128)(2,1)}, bf16[32,112,128]{2,1,0:T(8,128)(2,1)}) custom-call(s32[3072]{0:T(1024)} %bitcast.10, s32[4]{0:T(128)} %copy-done.5, bf16[192,256]{1,0:T(8,128)(2,1)} %copy-done, bf16[1152,3072]{1,0:T(8,128)(2,1)} %blocks.5, f32[7,32,128]{2,1,0:T(8,128)} %copy-done.4), custom_call_target="tpu_custom_call" | custom-call | bytes 90000000 | tf_op jit(solution)/shard_map/turned/pallas_call | solution.py:491
  40.3 7.6 %all-to-all-start.2 = ((bf16[32,496,128]{2,1,0:T(8,128)(2,1)}), bf16[32,496,128]{2,1,0:T(8,128)(2,1)}, u32[]{:S(2)}, u32[]{:S(2)}) async-start(bf16[32,496,128]{2,1,0:T(8,128)(2,1)} %get-tuple-element.53), calls=%async_computation.2 | async-start | bytes 8126464 | tf_op jit(solution)/shard_map/all_to_all | solution.py:522
  48.3 3.2 %collective-permute-done.2.other = bf16[16,384,128]{2,1,0:T(8,128)(2,1)S(1)} collective-permute-done((bf16[16,384,128]{2,1,0:T(8,128)(2,1)S(1)}, bf16[16,384,128]{2,1,0:T(8,128)(2,1)S(1)}, u32[]{:S(2)}, u32[]{:S(2)}) %collective-permute-start.2) | collective-permute-done | bytes 1572896 | tf_op jit(solution)/shard_map/ppermute | solution.py:524
  51.5 1.3 %answer.1 = (bf16[32,96,128]{2,1,0:T(8,128)(2,1)S(1)}, bf16[32,96,128]{2,1,0:T(8,128)(2,1)S(1)}) custom-call(s32[128,128]{1,0:T(8,128)S(1)} %collective-permute-done.from_lower, s32[128,128]{1,0:T(8,128)S(1)} %collective-permute-done.1.from_upper, bf16[16,384,128]{2,1,0:T(8,128)(2,1)S(1)} %all-to-all-done.1.same, ...), custom_call_target="tpu_custom_call" | custom-call | tf_op jit(solution)/shard_map/answer/pallas_call | solution.py:525
  52.8 2.0 %collective-permute-start.4 = (bf16[32,96,128]{2,1,0:T(8,128)(2,1)S(1)}, bf16[32,96,128]{2,1,0:T(8,128)(2,1)S(1)}, u32[]{:S(2)}, u32[]{:S(2)}) collective-permute-start(bf16[32,96,128]{2,1,0:T(8,128)(2,1)S(1)} %get-tuple-element.61), channel_id=1, source_target_pairs={{32,0},{64,32},{96,64},{0,96},{33,1},{65,33},{97,65},{1,97},{34,2}... | collective-permute-start | bytes 2359304 | tf_op jit(solution)/shard_map/ppermute | solution.py:436
  54.8 1.0 diagonal.1.local
  55.8 16.6 %collective-permute-done.3.lower = bf16[32,96,128]{2,1,0:T(8,128)(2,1)S(1)} collective-permute-done((bf16[32,96,128]{2,1,0:T(8,128)(2,1)S(1)}, bf16[32,96,128]{2,1,0:T(8,128)(2,1)S(1)}, u32[]{:S(2)}, u32[]{:S(2)}) %collective-permute-start.3) | collective-permute-done | bytes 786464 | tf_op jit(solution)/shard_map/ppermute | solution.py:436
  72.5 1.3 %collective-permute-done.4.upper = bf16[32,96,128]{2,1,0:T(8,128)(2,1)S(1)} collective-permute-done((bf16[32,96,128]{2,1,0:T(8,128)(2,1)S(1)}, bf16[32,96,128]{2,1,0:T(8,128)(2,1)S(1)}, u32[]{:S(2)}, u32[]{:S(2)}) %collective-permute-start.4) | collective-permute-done | bytes 786464 | tf_op jit(solution)/shard_map/ppermute | solution.py:436
  73.8 23.5 %pairs.1 = (f32[128,3072]{1,0:T(8,128)}, f32[384,256]{1,0:T(8,128)S(1)}) custom-call(s32[3072]{0:T(1024)S(1)} %bitcast.8, s32[3072]{0:T(1024)S(1)} %bitcast.9, s32[4]{0:T(128)S(1)} %copy-done.6, bf16[192,256]{1,0:T(8,128)(2,1)S(1)} %copy-done.1, bf16[1152,3072]{1,0:T(8,128)(2,1)} %blocks.5, s32[24,128]{1,0:T(8,128)S(1)} %get-tuple-element.56.half, ...), custom_call_target="tpu_custom_call" | custom-call | bytes 126000000 | tf_op jit(solution)/shard_map/pairs/pallas_call | solution.py:553
  97.3 2.7 %all-to-all-done.2.blocks = bf16[32,496,128]{2,1,0:T(8,128)(2,1)} async-done(((bf16[32,496,128]{2,1,0:T(8,128)(2,1)}), bf16[32,496,128]{2,1,0:T(8,128)(2,1)}, u32[]{:S(2)}, u32[]{:S(2)}) %all-to-all-start.2) | async-done | bytes 4063264 | tf_op jit(solution)/shard_map/all_to_all | solution.py:522
  100.0 6.9 %collect.1 = (bf16[256,384]{1,0:T(8,128)(2,1)S(1)}, f32[256,384]{1,0:T(8,128)S(1)}, bf16[256,384]{1,0:T(8,128)(2,1)S(1)}, s32[1]{0:T(128)}) custom-call(bf16[32,496,128]{2,1,0:T(8,128)(2,1)} %all-to-all-done.2.blocks), custom_call_target="tpu_custom_call" | custom-call | tf_op jit(solution)/shard_map/collect/pallas_call | solution.py:592
  107.6 2.0 %collective-permute-start.6 = (bf16[256,384]{1,0:T(8,128)(2,1)S(1)}, bf16[256,384]{1,0:T(8,128)(2,1)S(1)}, u32[]{:S(2)}, u32[]{:S(2)}) collective-permute-start(bf16[256,384]{1,0:T(8,128)(2,1)S(1)} %get-tuple-element.72), channel_id=1, source_target_pairs={{32,0},{64,32},{96,64},{0,96},{33,1},{65,33},{97,65},{1,97},{34,2}... | collective-permute-start | bytes 589832 | tf_op jit(solution)/shard_map/ppermute | solution.py:436
  109.6 3.6 %collective-permute-done.5.from_lower = bf16[256,384]{1,0:T(8,128)(2,1)S(1)} collective-permute-done((bf16[256,384]{1,0:T(8,128)(2,1)S(1)}, bf16[256,384]{1,0:T(8,128)(2,1)S(1)}, u32[]{:S(2)}, u32[]{:S(2)}) %collective-permute-start.5) | collective-permute-done | bytes 196640 | tf_op jit(solution)/shard_map/ppermute | solution.py:436
  113.3 1.3 %collective-permute-done.6.from_upper = bf16[256,384]{1,0:T(8,128)(2,1)S(1)} collective-permute-done((bf16[256,384]{1,0:T(8,128)(2,1)S(1)}, bf16[256,384]{1,0:T(8,128)(2,1)S(1)}, u32[]{:S(2)}, u32[]{:S(2)}) %collective-permute-start.6) | collective-permute-done | bytes 196640 | tf_op jit(solution)/shard_map/ppermute | solution.py:436
  114.5 1.7 %finish.1 = f32[384,256]{1,0:T(8,128)} custom-call(s32[4]{0:T(128)S(1)} %copy-done.6, f32[384,256]{1,0:T(8,128)S(1)} %get-tuple-element.63.total, f32[256,384]{1,0:T(8,128)S(1)} %get-tuple-element.70.here, bf16[256,384]{1,0:T(8,128)(2,1)S(1)} %collective-permute-done.5.from_lower, bf16[256,384]{1,0:T(8,128)(2,1)S(1)} %collective-permute-done.6.from_upper), custom_call_target="tpu_custom_call" | custom-call | tf_op jit(solution)/shard_map/finish/pallas_call | solution.py:619
  (22 shorter events, 0.6 us)
Async XLA Ops:
  0.6 1.1 copy-start.2
  3.2 0.6 copy-start
  3.8 8.9 %copy-start.8 = (s32[3072]{0:T(1024)S(1)}, s32[3072]{0:T(1024)}, u32[]{:S(2)}) copy-start(s32[3072]{0:T(1024)} %param.10) | copy-start | bytes 36868
  3.8 36.5 %all-to-all-start.1 = ((bf16[16,384,128]{2,1,0:T(8,128)(2,1)}), bf16[16,384,128]{2,1,0:T(8,128)(2,1)S(1)}, u32[]{:S(2)}, u32[]{:S(2)}) async-start(bf16[16,384,128]{2,1,0:T(8,128)(2,1)} %get-tuple-element.51), calls=%async_computation.1 | async-start | bytes 3145728 | tf_op jit(solution)/shard_map/all_to_all | solution.py:488
  12.7 7.7 %copy-start.5 = (s32[4]{0:T(128)}, s32[4]{0:T(128)S(1)}, u32[]{:S(2)}) copy-start(s32[4]{0:T(128)S(1)} %pad_add_fusion.info) | copy-start | bytes 52
  15.9 0.6 copy-start.4
  16.6 0.6 copy-start.7
  17.2 23.1 %collective-permute-start.1 = (s32[128,128]{1,0:T(8,128)S(1)}, s32[128,128]{1,0:T(8,128)S(1)}, u32[]{:S(2)}, u32[]{:S(2)}) collective-permute-start(s32[128,128]{1,0:T(8,128)S(1)} %get-tuple-element.52), channel_id=1, source_target_pairs={{32,0},{64,32},{96,64},{0,96},{33,1},{65,33},{97,65},{1,97},{34,2}... | collective-permute-start | bytes 196616 | tf_op jit(solution)/shard_map/ppermute | solution.py:436
  18.0 22.3 %collective-permute-start = (s32[128,128]{1,0:T(8,128)S(1)}, s32[128,128]{1,0:T(8,128)S(1)}, u32[]{:S(2)}, u32[]{:S(2)}) collective-permute-start(s32[128,128]{1,0:T(8,128)S(1)} %get-tuple-element.52), channel_id=1, source_target_pairs={{96,0},{0,32},{32,64},{64,96},{97,1},{1,33},{33,65},{65,97},{98,2}... | collective-permute-start | bytes 196616 | tf_op jit(solution)/shard_map/ppermute | solution.py:436
  40.3 59.7 %all-to-all-start.2 = ((bf16[32,496,128]{2,1,0:T(8,128)(2,1)}), bf16[32,496,128]{2,1,0:T(8,128)(2,1)}, u32[]{:S(2)}, u32[]{:S(2)}) async-start(bf16[32,496,128]{2,1,0:T(8,128)(2,1)} %get-tuple-element.53), calls=%async_computation.2 | async-start | bytes 8126464 | tf_op jit(solution)/shard_map/all_to_all | solution.py:522
  48.0 6.9 %copy-start.1 = (bf16[192,256]{1,0:T(8,128)(2,1)S(1)}, bf16[192,256]{1,0:T(8,128)(2,1)}, u32[]{:S(2)}) copy-start(bf16[192,256]{1,0:T(8,128)(2,1)} %copy-done) | copy-start | bytes 294916
  48.0 6.9 %copy-start.3 = (bf16[1152,256]{1,0:T(8,128)(2,1)S(1)}, bf16[1152,256]{1,0:T(8,128)(2,1)}, u32[]{:S(2)}) copy-start(bf16[1152,256]{1,0:T(8,128)(2,1)} %blocks.4) | copy-start | bytes 1769476
  48.0 25.8 %copy-start.6 = (s32[4]{0:T(128)S(1)}, s32[4]{0:T(128)}, u32[]{:S(2)}) copy-start(s32[4]{0:T(128)} %copy-done.5) | copy-start | bytes 52
  48.0 3.5 %collective-permute-start.2 = (bf16[16,384,128]{2,1,0:T(8,128)(2,1)S(1)}, bf16[16,384,128]{2,1,0:T(8,128)(2,1)S(1)}, u32[]{:S(2)}, u32[]{:S(2)}) collective-permute-start(bf16[16,384,128]{2,1,0:T(8,128)(2,1)S(1)} %all-to-all-done.1.same), channel_id=1, source_target_pairs={{1,0},{0,1},{3,2},{2,3},{5,4},{4,5},{7,6},{6,7},{9,8},{8,9},{11,10... | collective-permute-start | bytes 4718600 | tf_op jit(solution)/shard_map/ppermute | solution.py:524
  52.7 19.7 %collective-permute-start.3 = (bf16[32,96,128]{2,1,0:T(8,128)(2,1)S(1)}, bf16[32,96,128]{2,1,0:T(8,128)(2,1)S(1)}, u32[]{:S(2)}, u32[]{:S(2)}) collective-permute-start(bf16[32,96,128]{2,1,0:T(8,128)(2,1)S(1)} %get-tuple-element.60), channel_id=1, source_target_pairs={{96,0},{0,32},{32,64},{64,96},{97,1},{1,33},{33,65},{65,97},{98,2}... | collective-permute-start | bytes 2359304 | tf_op jit(solution)/shard_map/ppermute | solution.py:436
  52.8 20.9 %collective-permute-start.4 = (bf16[32,96,128]{2,1,0:T(8,128)(2,1)S(1)}, bf16[32,96,128]{2,1,0:T(8,128)(2,1)S(1)}, u32[]{:S(2)}, u32[]{:S(2)}) collective-permute-start(bf16[32,96,128]{2,1,0:T(8,128)(2,1)S(1)} %get-tuple-element.61), channel_id=1, source_target_pairs={{32,0},{64,32},{96,64},{0,96},{33,1},{65,33},{97,65},{1,97},{34,2}... | collective-permute-start | bytes 2359304 | tf_op jit(solution)/shard_map/ppermute | solution.py:436
  107.5 5.7 %collective-permute-start.5 = (bf16[256,384]{1,0:T(8,128)(2,1)S(1)}, bf16[256,384]{1,0:T(8,128)(2,1)S(1)}, u32[]{:S(2)}, u32[]{:S(2)}) collective-permute-start(bf16[256,384]{1,0:T(8,128)(2,1)S(1)} %get-tuple-element.71), channel_id=1, source_target_pairs={{96,0},{0,32},{32,64},{64,96},{97,1},{1,33},{33,65},{65,97},{98,2}... | collective-permute-start | bytes 589832 | tf_op jit(solution)/shard_map/ppermute | solution.py:436
  107.6 6.9 %collective-permute-start.6 = (bf16[256,384]{1,0:T(8,128)(2,1)S(1)}, bf16[256,384]{1,0:T(8,128)(2,1)S(1)}, u32[]{:S(2)}, u32[]{:S(2)}) collective-permute-start(bf16[256,384]{1,0:T(8,128)(2,1)S(1)} %get-tuple-element.72), channel_id=1, source_target_pairs={{32,0},{64,32},{96,64},{0,96},{33,1},{65,33},{97,65},{1,97},{34,2}... | collective-permute-start | bytes 589832 | tf_op jit(solution)/shard_map/ppermute | solution.py:436

commit v4 on v3

--- a/solution.py
+++ b/solution.py
@@ -460,7 +460,7 @@
         out_shape=(shape((FEAT, mols), bf16), shape((CHIPS, held_rows, LANES), bf16)),
         in_specs=[VMEM],
         out_specs=(VMEM,) * 2,
-        compiler_params=params(),
+        compiler_params=params(60),
         name="predict",
     )(history)
 

time: 117 us -> 116 us (level)
  local copies, waits for them, and re-layouts: 3.02 us -> 1.26 us
    unnamed x18 -> x14, local copies, waits for them, and re-layouts: 3.02 us -> 1.26 us
where the time goes in v4:
time: 116 us
  Pallas kernels  59.9 us (52%)
  waiting for transfers between devices  28.8 us (25%)
  starting transfers between devices  23.5 us (20%)
  between operations  2.08 us (2%)
  local copies, waits for them, and re-layouts  1.26 us (1%)
    pallas_call x1, Pallas kernels, on_device(): pl.pallas_call(functools.partial(pairs_kernel, per_mol), grid=(pairs // B...  23.5 us
    ppermute x6, waiting for transfers between devices, shifted(): return lax.ppermute(block, axis, route)  22.9 us
    pallas_call x1, Pallas kernels, on_device(): pl.pallas_call(functools.partial(turned_kernel, per_mol), grid=(pairs //...  19.9 us
    all_to_all x1, starting transfers between devices, on_device(): lax.all_to_all(rows, 'sub', 0, 0, tiled=True, axis_index_groups=cores)  8.18 us
    all_to_all x1, starting transfers between devices, on_device(): received = lax.all_to_all(payload, 'sub', 0, 0, tiled=True)  7.64 us
    ppermute x6, starting transfers between devices, shifted(): return lax.ppermute(block, axis, route)  7.42 us
    pallas_call x1, Pallas kernels, on_device(): pl.pallas_call(collect_kernel, grid=(teams // group,), out_shape=sums_sha...  6.86 us
    ppermute x1, waiting for transfers between devices, on_device(): other = lax.ppermute(same, 'sub', [(i ^ 1, i) for i in range(teams)])  3.2 us
  transfers between devices with their start and end apart: 9, of which 6 were waited for; matrix products, arithmetic and copies ran while one was open for 0% of the time, Pallas kernels for 42%

profile of v4, /device:TPU:6, one launch (start us, length us, event | category | flops | bytes accessed | tf_op | source)
XLA Modules:
  0.0 115.7 jit_solution(15261008213815378946)
XLA Ops:
  0.6 2.5 %predict.1 = (bf16[192,256]{1,0:T(8,128)(2,1)}, bf16[16,384,128]{2,1,0:T(8,128)(2,1)}) custom-call(f32[4,192,256]{2,1,0:T(8,128)} %history.1), custom_call_target="tpu_custom_call" | custom-call | tf_op jit(solution)/shard_map/predict/pallas_call | solution.py:458
  3.2 8.2 %all-to-all-start.1 = ((bf16[16,384,128]{2,1,0:T(8,128)(2,1)}), bf16[16,384,128]{2,1,0:T(8,128)(2,1)S(1)}, u32[]{:S(2)}, u32[]{:S(2)}) async-start(bf16[16,384,128]{2,1,0:T(8,128)(2,1)} %get-tuple-element.51), calls=%async_computation.1 | async-start | bytes 3145728 | tf_op jit(solution)/shard_map/all_to_all | solution.py:488
  12.1 3.2 %rank.1 = (s32[24,128]{1,0:T(8,128)S(1)}, s32[24,128]{1,0:T(8,128)S(1)}, s32[24,128]{1,0:T(8,128)S(1)}, s32[24,128]{1,0:T(8,128)S(1)}, s32[128,128]{1,0:T(8,128)S(1)}, /*index=5*/f32[7,32,128]{2,1,0:T(8,128)S(1)}) custom-call(s32[4]{0:T(128)S(1)} %pad_add_fusion.info, s32[24,128]{1,0:T(8,128)S(1)} %bitcast.11), custom_call_target="tpu_custom_call" | custom-call | bytes 10800000 | tf_op jit(solution)/shard_map/rank/pallas_call | solution.py:468
  15.3 0.6 copy-done.2
  15.9 0.6 copy-done.5
  16.5 0.8 collective-permute-start.1
  17.4 2.4 %collective-permute-start = (s32[128,128]{1,0:T(8,128)S(1)}, s32[128,128]{1,0:T(8,128)S(1)}, u32[]{:S(2)}, u32[]{:S(2)}) collective-permute-start(s32[128,128]{1,0:T(8,128)S(1)} %get-tuple-element.52), channel_id=1, source_target_pairs={{96,0},{0,32},{32,64},{64,96},{97,1},{1,33},{33,65},{65,97},{98,2}... | collective-permute-start | bytes 196616 | tf_op jit(solution)/shard_map/ppermute | solution.py:436
  19.8 19.9 %turned.1 = (bf16[32,496,128]{2,1,0:T(8,128)(2,1)}, bf16[32,112,128]{2,1,0:T(8,128)(2,1)}) custom-call(s32[3072]{0:T(1024)} %bitcast.10, s32[4]{0:T(128)} %copy-done.3, bf16[192,256]{1,0:T(8,128)(2,1)} %get-tuple-element.48.guess, bf16[1152,3072]{1,0:T(8,128)(2,1)} %blocks.5, f32[7,32,128]{2,1,0:T(8,128)} %copy-done.2), custom_call_target="tpu_custom_call" | custom-call | bytes 90000000 | tf_op jit(solution)/shard_map/turned/pallas_call | solution.py:491
  39.7 7.6 %all-to-all-start.2 = ((bf16[32,496,128]{2,1,0:T(8,128)(2,1)}), bf16[32,496,128]{2,1,0:T(8,128)(2,1)}, u32[]{:S(2)}, u32[]{:S(2)}) async-start(bf16[32,496,128]{2,1,0:T(8,128)(2,1)} %get-tuple-element.53), calls=%async_computation.2 | async-start | bytes 8126464 | tf_op jit(solution)/shard_map/all_to_all | solution.py:522
  47.4 0.3 collective-permute-start.2
  47.6 3.2 %collective-permute-done.2.other = bf16[16,384,128]{2,1,0:T(8,128)(2,1)S(1)} collective-permute-done((bf16[16,384,128]{2,1,0:T(8,128)(2,1)S(1)}, bf16[16,384,128]{2,1,0:T(8,128)(2,1)S(1)}, u32[]{:S(2)}, u32[]{:S(2)}) %collective-permute-start.2) | collective-permute-done | bytes 1572896 | tf_op jit(solution)/shard_map/ppermute | solution.py:524
  50.9 1.3 %answer.1 = (bf16[32,96,128]{2,1,0:T(8,128)(2,1)S(1)}, bf16[32,96,128]{2,1,0:T(8,128)(2,1)S(1)}) custom-call(s32[128,128]{1,0:T(8,128)S(1)} %collective-permute-done.from_lower, s32[128,128]{1,0:T(8,128)S(1)} %collective-permute-done.1.from_upper, bf16[16,384,128]{2,1,0:T(8,128)(2,1)S(1)} %all-to-all-done.1.same, ...), custom_call_target="tpu_custom_call" | custom-call | tf_op jit(solution)/shard_map/answer/pallas_call | solution.py:525
  52.2 2.0 %collective-permute-start.4 = (bf16[32,96,128]{2,1,0:T(8,128)(2,1)S(1)}, bf16[32,96,128]{2,1,0:T(8,128)(2,1)S(1)}, u32[]{:S(2)}, u32[]{:S(2)}) collective-permute-start(bf16[32,96,128]{2,1,0:T(8,128)(2,1)S(1)} %get-tuple-element.61), channel_id=1, source_target_pairs={{32,0},{64,32},{96,64},{0,96},{33,1},{65,33},{97,65},{1,97},{34,2}... | collective-permute-start | bytes 2359304 | tf_op jit(solution)/shard_map/ppermute | solution.py:436
  54.2 1.0 diagonal.1.local
  55.2 16.6 %collective-permute-done.3.lower = bf16[32,96,128]{2,1,0:T(8,128)(2,1)S(1)} collective-permute-done((bf16[32,96,128]{2,1,0:T(8,128)(2,1)S(1)}, bf16[32,96,128]{2,1,0:T(8,128)(2,1)S(1)}, u32[]{:S(2)}, u32[]{:S(2)}) %collective-permute-start.3) | collective-permute-done | bytes 786464 | tf_op jit(solution)/shard_map/ppermute | solution.py:436
  71.8 1.3 %collective-permute-done.4.upper = bf16[32,96,128]{2,1,0:T(8,128)(2,1)S(1)} collective-permute-done((bf16[32,96,128]{2,1,0:T(8,128)(2,1)S(1)}, bf16[32,96,128]{2,1,0:T(8,128)(2,1)S(1)}, u32[]{:S(2)}, u32[]{:S(2)}) %collective-permute-start.4) | collective-permute-done | bytes 786464 | tf_op jit(solution)/shard_map/ppermute | solution.py:436
  73.1 23.5 %pairs.1 = (f32[128,3072]{1,0:T(8,128)}, f32[384,256]{1,0:T(8,128)S(1)}) custom-call(s32[3072]{0:T(1024)S(1)} %bitcast.8, s32[3072]{0:T(1024)S(1)} %bitcast.9, s32[4]{0:T(128)S(1)} %copy-done.4, bf16[192,256]{1,0:T(8,128)(2,1)S(1)} %copy-done, bf16[1152,3072]{1,0:T(8,128)(2,1)} %blocks.5, s32[24,128]{1,0:T(8,128)S(1)} %get-tuple-element.56.half, ...), custom_call_target="tpu_custom_call" | custom-call | bytes 126000000 | tf_op jit(solution)/shard_map/pairs/pallas_call | solution.py:553
  96.6 2.7 %all-to-all-done.2.blocks = bf16[32,496,128]{2,1,0:T(8,128)(2,1)} async-done(((bf16[32,496,128]{2,1,0:T(8,128)(2,1)}), bf16[32,496,128]{2,1,0:T(8,128)(2,1)}, u32[]{:S(2)}, u32[]{:S(2)}) %all-to-all-start.2) | async-done | bytes 4063264 | tf_op jit(solution)/shard_map/all_to_all | solution.py:522
  99.4 6.9 %collect.1 = (bf16[256,384]{1,0:T(8,128)(2,1)S(1)}, f32[256,384]{1,0:T(8,128)S(1)}, bf16[256,384]{1,0:T(8,128)(2,1)S(1)}, s32[1]{0:T(128)}) custom-call(bf16[32,496,128]{2,1,0:T(8,128)(2,1)} %all-to-all-done.2.blocks), custom_call_target="tpu_custom_call" | custom-call | tf_op jit(solution)/shard_map/collect/pallas_call | solution.py:592
  106.9 0.1 collective-permute-start.5
  107.0 2.0 %collective-permute-start.6 = (bf16[256,384]{1,0:T(8,128)(2,1)S(1)}, bf16[256,384]{1,0:T(8,128)(2,1)S(1)}, u32[]{:S(2)}, u32[]{:S(2)}) collective-permute-start(bf16[256,384]{1,0:T(8,128)(2,1)S(1)} %get-tuple-element.72), channel_id=1, source_target_pairs={{32,0},{64,32},{96,64},{0,96},{33,1},{65,33},{97,65},{1,97},{34,2}... | collective-permute-start | bytes 589832 | tf_op jit(solution)/shard_map/ppermute | solution.py:436
  109.0 3.6 %collective-permute-done.5.from_lower = bf16[256,384]{1,0:T(8,128)(2,1)S(1)} collective-permute-done((bf16[256,384]{1,0:T(8,128)(2,1)S(1)}, bf16[256,384]{1,0:T(8,128)(2,1)S(1)}, u32[]{:S(2)}, u32[]{:S(2)}) %collective-permute-start.5) | collective-permute-done | bytes 196640 | tf_op jit(solution)/shard_map/ppermute | solution.py:436
  112.6 1.3 %collective-permute-done.6.from_upper = bf16[256,384]{1,0:T(8,128)(2,1)S(1)} collective-permute-done((bf16[256,384]{1,0:T(8,128)(2,1)S(1)}, bf16[256,384]{1,0:T(8,128)(2,1)S(1)}, u32[]{:S(2)}, u32[]{:S(2)}) %collective-permute-start.6) | collective-permute-done | bytes 196640 | tf_op jit(solution)/shard_map/ppermute | solution.py:436
  113.9 1.7 %finish.1 = f32[384,256]{1,0:T(8,128)} custom-call(s32[4]{0:T(128)S(1)} %copy-done.4, f32[384,256]{1,0:T(8,128)S(1)} %get-tuple-element.63.total, f32[256,384]{1,0:T(8,128)S(1)} %get-tuple-element.70.here, bf16[256,384]{1,0:T(8,128)(2,1)S(1)} %collective-permute-done.5.from_lower, bf16[256,384]{1,0:T(8,128)(2,1)S(1)} %collective-permute-done.6.from_upper), custom_call_target="tpu_custom_call" | custom-call | tf_op jit(solution)/shard_map/finish/pallas_call | solution.py:619
  (18 shorter events, 0.2 us)
Async XLA Ops:
  3.2 8.9 %copy-start.6 = (s32[3072]{0:T(1024)S(1)}, s32[3072]{0:T(1024)}, u32[]{:S(2)}) copy-start(s32[3072]{0:T(1024)} %param.10) | copy-start | bytes 36868
  3.2 36.5 %all-to-all-start.1 = ((bf16[16,384,128]{2,1,0:T(8,128)(2,1)}), bf16[16,384,128]{2,1,0:T(8,128)(2,1)S(1)}, u32[]{:S(2)}, u32[]{:S(2)}) async-start(bf16[16,384,128]{2,1,0:T(8,128)(2,1)} %get-tuple-element.51), calls=%async_computation.1 | async-start | bytes 3145728 | tf_op jit(solution)/shard_map/all_to_all | solution.py:488
  12.1 7.7 %copy-start.3 = (s32[4]{0:T(128)}, s32[4]{0:T(128)S(1)}, u32[]{:S(2)}) copy-start(s32[4]{0:T(128)S(1)} %pad_add_fusion.info) | copy-start | bytes 52
  15.3 0.6 copy-start.2
  15.9 0.6 copy-start.5
  16.5 23.1 %collective-permute-start.1 = (s32[128,128]{1,0:T(8,128)S(1)}, s32[128,128]{1,0:T(8,128)S(1)}, u32[]{:S(2)}, u32[]{:S(2)}) collective-permute-start(s32[128,128]{1,0:T(8,128)S(1)} %get-tuple-element.52), channel_id=1, source_target_pairs={{32,0},{64,32},{96,64},{0,96},{33,1},{65,33},{97,65},{1,97},{34,2}... | collective-permute-start | bytes 196616 | tf_op jit(solution)/shard_map/ppermute | solution.py:436
  17.4 22.3 %collective-permute-start = (s32[128,128]{1,0:T(8,128)S(1)}, s32[128,128]{1,0:T(8,128)S(1)}, u32[]{:S(2)}, u32[]{:S(2)}) collective-permute-start(s32[128,128]{1,0:T(8,128)S(1)} %get-tuple-element.52), channel_id=1, source_target_pairs={{96,0},{0,32},{32,64},{64,96},{97,1},{1,33},{33,65},{65,97},{98,2}... | collective-permute-start | bytes 196616 | tf_op jit(solution)/shard_map/ppermute | solution.py:436
  39.7 59.7 %all-to-all-start.2 = ((bf16[32,496,128]{2,1,0:T(8,128)(2,1)}), bf16[32,496,128]{2,1,0:T(8,128)(2,1)}, u32[]{:S(2)}, u32[]{:S(2)}) async-start(bf16[32,496,128]{2,1,0:T(8,128)(2,1)} %get-tuple-element.53), calls=%async_computation.2 | async-start | bytes 8126464 | tf_op jit(solution)/shard_map/all_to_all | solution.py:522
  47.3 6.9 %copy-start = (bf16[192,256]{1,0:T(8,128)(2,1)S(1)}, bf16[192,256]{1,0:T(8,128)(2,1)}, u32[]{:S(2)}) copy-start(bf16[192,256]{1,0:T(8,128)(2,1)} %get-tuple-element.48.guess) | copy-start | bytes 294916
  47.3 6.9 %copy-start.1 = (bf16[1152,256]{1,0:T(8,128)(2,1)S(1)}, bf16[1152,256]{1,0:T(8,128)(2,1)}, u32[]{:S(2)}) copy-start(bf16[1152,256]{1,0:T(8,128)(2,1)} %blocks.4) | copy-start | bytes 1769476
  47.3 25.8 %copy-start.4 = (s32[4]{0:T(128)S(1)}, s32[4]{0:T(128)}, u32[]{:S(2)}) copy-start(s32[4]{0:T(128)} %copy-done.3) | copy-start | bytes 52
  47.4 3.5 %collective-permute-start.2 = (bf16[16,384,128]{2,1,0:T(8,128)(2,1)S(1)}, bf16[16,384,128]{2,1,0:T(8,128)(2,1)S(1)}, u32[]{:S(2)}, u32[]{:S(2)}) collective-permute-start(bf16[16,384,128]{2,1,0:T(8,128)(2,1)S(1)} %all-to-all-done.1.same), channel_id=1, source_target_pairs={{1,0},{0,1},{3,2},{2,3},{5,4},{4,5},{7,6},{6,7},{9,8},{8,9},{11,10... | collective-permute-start | bytes 4718600 | tf_op jit(solution)/shard_map/ppermute | solution.py:524
  52.1 19.7 %collective-permute-start.3 = (bf16[32,96,128]{2,1,0:T(8,128)(2,1)S(1)}, bf16[32,96,128]{2,1,0:T(8,128)(2,1)S(1)}, u32[]{:S(2)}, u32[]{:S(2)}) collective-permute-start(bf16[32,96,128]{2,1,0:T(8,128)(2,1)S(1)} %get-tuple-element.60), channel_id=1, source_target_pairs={{96,0},{0,32},{32,64},{64,96},{97,1},{1,33},{33,65},{65,97},{98,2}... | collective-permute-start | bytes 2359304 | tf_op jit(solution)/shard_map/ppermute | solution.py:436
  52.2 20.9 %collective-permute-start.4 = (bf16[32,96,128]{2,1,0:T(8,128)(2,1)S(1)}, bf16[32,96,128]{2,1,0:T(8,128)(2,1)S(1)}, u32[]{:S(2)}, u32[]{:S(2)}) collective-permute-start(bf16[32,96,128]{2,1,0:T(8,128)(2,1)S(1)} %get-tuple-element.61), channel_id=1, source_target_pairs={{32,0},{64,32},{96,64},{0,96},{33,1},{65,33},{97,65},{1,97},{34,2}... | collective-permute-start | bytes 2359304 | tf_op jit(solution)/shard_map/ppermute | solution.py:436
  106.9 5.7 %collective-permute-start.5 = (bf16[256,384]{1,0:T(8,128)(2,1)S(1)}, bf16[256,384]{1,0:T(8,128)(2,1)S(1)}, u32[]{:S(2)}, u32[]{:S(2)}) collective-permute-start(bf16[256,384]{1,0:T(8,128)(2,1)S(1)} %get-tuple-element.71), channel_id=1, source_target_pairs={{96,0},{0,32},{32,64},{64,96},{97,1},{1,33},{33,65},{65,97},{98,2}... | collective-permute-start | bytes 589832 | tf_op jit(solution)/shard_map/ppermute | solution.py:436
  107.0 6.9 %collective-permute-start.6 = (bf16[256,384]{1,0:T(8,128)(2,1)S(1)}, bf16[256,384]{1,0:T(8,128)(2,1)S(1)}, u32[]{:S(2)}, u32[]{:S(2)}) collective-permute-start(bf16[256,384]{1,0:T(8,128)(2,1)S(1)} %get-tuple-element.72), channel_id=1, source_target_pairs={{32,0},{64,32},{96,64},{0,96},{33,1},{65,33},{97,65},{1,97},{34,2}... | collective-permute-start | bytes 589832 | tf_op jit(solution)/shard_map/ppermute | solution.py:436

commit v5 on v4

--- a/solution.py
+++ b/solution.py
@@ -478,7 +478,7 @@
             pltpu.VMEM((2 * teams, pairs), bf16),
             pltpu.VMEM((2 * LANES, pairs), bf16),
         ],
-        compiler_params=params(),
+        compiler_params=params(60),
         cost_estimate=cost(3),
         name="rank",
     )(info, neighbours.reshape(columns, LANES))

time: 116 us -> 116 us (level)
  local copies, waits for them, and re-layouts: 1.26 us -> 0.03 us
    unnamed x14 -> x12, local copies, waits for them, and re-layouts: 1.26 us -> 0.03 us
  transfers between devices with their start and end apart: 9 -> 9, of which waited for: 6 -> 6; matrix products, arithmetic and copies ran while one was open for 0% -> 1% of each run, Pallas kernels for 42% -> 43%
where the time goes in v5:
time: 116 us
  Pallas kernels  60.8 us (52%)
  waiting for transfers between devices  28.7 us (25%)
  starting transfers between devices  23.4 us (20%)
  between operations  2.09 us (2%)
    pallas_call x1, Pallas kernels, on_device(): pl.pallas_call(functools.partial(pairs_kernel, per_mol), grid=(pairs // B...  23.5 us
    ppermute x6, waiting for transfers between devices, shifted(): return lax.ppermute(block, axis, route)  22.9 us
    pallas_call x1, Pallas kernels, on_device(): pl.pallas_call(functools.partial(turned_kernel, per_mol), grid=(pairs //...  19.9 us
    all_to_all x1, starting transfers between devices, on_device(): lax.all_to_all(rows, 'sub', 0, 0, tiled=True, axis_index_groups=cores)  8.05 us
    all_to_all x1, starting transfers between devices, on_device(): received = lax.all_to_all(payload, 'sub', 0, 0, tiled=True)  7.62 us
    ppermute x6, starting transfers between devices, shifted(): return lax.ppermute(block, axis, route)  7.42 us
    pallas_call x1, Pallas kernels, on_device(): pl.pallas_call(collect_kernel, grid=(teams // group,), out_shape=sums_sha...  6.86 us
    pallas_call x1, Pallas kernels, on_device(): pl.pallas_call(functools.partial(rank_kernel, teams, domains, mols), out_...  3.97 us
  transfers between devices with their start and end apart: 9, of which 6 were waited for; matrix products, arithmetic and copies ran while one was open for 1% of the time, Pallas kernels for 43%

profile of v5, /device:TPU:6, one launch (start us, length us, event | category | flops | bytes accessed | tf_op | source)
XLA Modules:
  0.0 115.6 jit_solution(2748501613983699099)
XLA Ops:
  0.6 2.5 %predict.1 = (bf16[192,256]{1,0:T(8,128)(2,1)}, bf16[16,384,128]{2,1,0:T(8,128)(2,1)}) custom-call(f32[4,192,256]{2,1,0:T(8,128)} %history.1), custom_call_target="tpu_custom_call" | custom-call | tf_op jit(solution)/shard_map/predict/pallas_call | solution.py:458
  3.2 8.0 %all-to-all-start.1 = ((bf16[16,384,128]{2,1,0:T(8,128)(2,1)}), bf16[16,384,128]{2,1,0:T(8,128)(2,1)S(1)}, u32[]{:S(2)}, u32[]{:S(2)}) async-start(bf16[16,384,128]{2,1,0:T(8,128)(2,1)} %get-tuple-element.51), calls=%async_computation.1 | async-start | bytes 3145728 | tf_op jit(solution)/shard_map/all_to_all | solution.py:488
  11.9 0.6 pad_add_fusion.info
  12.5 4.0 %rank.1 = (s32[24,128]{1,0:T(8,128)}, s32[24,128]{1,0:T(8,128)}, s32[24,128]{1,0:T(8,128)}, s32[24,128]{1,0:T(8,128)}, s32[128,128]{1,0:T(8,128)}, /*index=5*/f32[7,32,128]{2,1,0:T(8,128)}) custom-call(s32[4]{0:T(128)} %pad_add_fusion.info, s32[24,128]{1,0:T(8,128)} %bitcast.11), custom_call_target="tpu_custom_call" | custom-call | bytes 10800000 | tf_op jit(solution)/shard_map/rank/pallas_call | solution.py:468
  16.5 0.8 collective-permute-start.1
  17.3 2.4 %collective-permute-start = (s32[128,128]{1,0:T(8,128)}, s32[128,128]{1,0:T(8,128)S(1)}, u32[]{:S(2)}, u32[]{:S(2)}) collective-permute-start(s32[128,128]{1,0:T(8,128)} %get-tuple-element.52), channel_id=1, source_target_pairs={{96,0},{0,32},{32,64},{64,96},{97,1},{1,33},{33,65},{65,97},{98,2}... | collective-permute-start | bytes 196616 | tf_op jit(solution)/shard_map/ppermute | solution.py:436
  19.7 19.9 %turned.1 = (bf16[32,496,128]{2,1,0:T(8,128)(2,1)}, bf16[32,112,128]{2,1,0:T(8,128)(2,1)}) custom-call(s32[3072]{0:T(1024)} %bitcast.10, s32[4]{0:T(128)} %pad_add_fusion.info, bf16[192,256]{1,0:T(8,128)(2,1)} %get-tuple-element.48.guess, bf16[1152,3072]{1,0:T(8,128)(2,1)} %blocks.5, f32[7,32,128]{2,1,0:T(8,128)} %get-tuple-element.49.label), custom_call_target="tpu_custom_call" | custom-call | bytes 90000000 | tf_op jit(solution)/shard_map/turned/pallas_call | solution.py:491
  39.6 7.6 %all-to-all-start.2 = ((bf16[32,496,128]{2,1,0:T(8,128)(2,1)}), bf16[32,496,128]{2,1,0:T(8,128)(2,1)}, u32[]{:S(2)}, u32[]{:S(2)}) async-start(bf16[32,496,128]{2,1,0:T(8,128)(2,1)} %get-tuple-element.53), calls=%async_computation.2 | async-start | bytes 8126464 | tf_op jit(solution)/shard_map/all_to_all | solution.py:522
  47.3 0.3 collective-permute-start.2
  47.6 3.2 %collective-permute-done.2.other = bf16[16,384,128]{2,1,0:T(8,128)(2,1)S(1)} collective-permute-done((bf16[16,384,128]{2,1,0:T(8,128)(2,1)S(1)}, bf16[16,384,128]{2,1,0:T(8,128)(2,1)S(1)}, u32[]{:S(2)}, u32[]{:S(2)}) %collective-permute-start.2) | collective-permute-done | bytes 1572896 | tf_op jit(solution)/shard_map/ppermute | solution.py:524
  50.8 1.3 %answer.1 = (bf16[32,96,128]{2,1,0:T(8,128)(2,1)S(1)}, bf16[32,96,128]{2,1,0:T(8,128)(2,1)S(1)}) custom-call(s32[128,128]{1,0:T(8,128)S(1)} %collective-permute-done.from_lower, s32[128,128]{1,0:T(8,128)S(1)} %collective-permute-done.1.from_upper, bf16[16,384,128]{2,1,0:T(8,128)(2,1)S(1)} %all-to-all-done.1.same, ...), custom_call_target="tpu_custom_call" | custom-call | tf_op jit(solution)/shard_map/answer/pallas_call | solution.py:525
  52.1 0.1 collective-permute-start.3
  52.1 2.0 %collective-permute-start.4 = (bf16[32,96,128]{2,1,0:T(8,128)(2,1)S(1)}, bf16[32,96,128]{2,1,0:T(8,128)(2,1)S(1)}, u32[]{:S(2)}, u32[]{:S(2)}) collective-permute-start(bf16[32,96,128]{2,1,0:T(8,128)(2,1)S(1)} %get-tuple-element.61), channel_id=1, source_target_pairs={{32,0},{64,32},{96,64},{0,96},{33,1},{65,33},{97,65},{1,97},{34,2}... | collective-permute-start | bytes 2359304 | tf_op jit(solution)/shard_map/ppermute | solution.py:436
  54.2 1.0 diagonal.1.local
  55.2 16.6 %collective-permute-done.3.lower = bf16[32,96,128]{2,1,0:T(8,128)(2,1)S(1)} collective-permute-done((bf16[32,96,128]{2,1,0:T(8,128)(2,1)S(1)}, bf16[32,96,128]{2,1,0:T(8,128)(2,1)S(1)}, u32[]{:S(2)}, u32[]{:S(2)}) %collective-permute-start.3) | collective-permute-done | bytes 786464 | tf_op jit(solution)/shard_map/ppermute | solution.py:436
  71.8 1.3 %collective-permute-done.4.upper = bf16[32,96,128]{2,1,0:T(8,128)(2,1)S(1)} collective-permute-done((bf16[32,96,128]{2,1,0:T(8,128)(2,1)S(1)}, bf16[32,96,128]{2,1,0:T(8,128)(2,1)S(1)}, u32[]{:S(2)}, u32[]{:S(2)}) %collective-permute-start.4) | collective-permute-done | bytes 786464 | tf_op jit(solution)/shard_map/ppermute | solution.py:436
  73.1 23.5 %pairs.1 = (f32[128,3072]{1,0:T(8,128)}, f32[384,256]{1,0:T(8,128)S(1)}) custom-call(s32[3072]{0:T(1024)S(1)} %bitcast.8, s32[3072]{0:T(1024)S(1)} %bitcast.9, s32[4]{0:T(128)S(1)} %copy-done.2, bf16[192,256]{1,0:T(8,128)(2,1)S(1)} %copy-done, bf16[1152,3072]{1,0:T(8,128)(2,1)} %blocks.5, s32[24,128]{1,0:T(8,128)S(1)} %copy-done.5, ...), custom_call_target="tpu_custom_call" | custom-call | bytes 126000000 | tf_op jit(solution)/shard_map/pairs/pallas_call | solution.py:553
  96.6 2.6 %all-to-all-done.2.blocks = bf16[32,496,128]{2,1,0:T(8,128)(2,1)} async-done(((bf16[32,496,128]{2,1,0:T(8,128)(2,1)}), bf16[32,496,128]{2,1,0:T(8,128)(2,1)}, u32[]{:S(2)}, u32[]{:S(2)}) %all-to-all-start.2) | async-done | bytes 4063264 | tf_op jit(solution)/shard_map/all_to_all | solution.py:522
  99.3 6.9 %collect.1 = (bf16[256,384]{1,0:T(8,128)(2,1)S(1)}, f32[256,384]{1,0:T(8,128)S(1)}, bf16[256,384]{1,0:T(8,128)(2,1)S(1)}, s32[1]{0:T(128)}) custom-call(bf16[32,496,128]{2,1,0:T(8,128)(2,1)} %all-to-all-done.2.blocks), custom_call_target="tpu_custom_call" | custom-call | tf_op jit(solution)/shard_map/collect/pallas_call | solution.py:592
  106.8 0.1 collective-permute-start.5
  106.9 2.0 %collective-permute-start.6 = (bf16[256,384]{1,0:T(8,128)(2,1)S(1)}, bf16[256,384]{1,0:T(8,128)(2,1)S(1)}, u32[]{:S(2)}, u32[]{:S(2)}) collective-permute-start(bf16[256,384]{1,0:T(8,128)(2,1)S(1)} %get-tuple-element.72), channel_id=1, source_target_pairs={{32,0},{64,32},{96,64},{0,96},{33,1},{65,33},{97,65},{1,97},{34,2}... | collective-permute-start | bytes 589832 | tf_op jit(solution)/shard_map/ppermute | solution.py:436
  108.9 3.6 %collective-permute-done.5.from_lower = bf16[256,384]{1,0:T(8,128)(2,1)S(1)} collective-permute-done((bf16[256,384]{1,0:T(8,128)(2,1)S(1)}, bf16[256,384]{1,0:T(8,128)(2,1)S(1)}, u32[]{:S(2)}, u32[]{:S(2)}) %collective-permute-start.5) | collective-permute-done | bytes 196640 | tf_op jit(solution)/shard_map/ppermute | solution.py:436
  112.5 1.3 %collective-permute-done.6.from_upper = bf16[256,384]{1,0:T(8,128)(2,1)S(1)} collective-permute-done((bf16[256,384]{1,0:T(8,128)(2,1)S(1)}, bf16[256,384]{1,0:T(8,128)(2,1)S(1)}, u32[]{:S(2)}, u32[]{:S(2)}) %collective-permute-start.6) | collective-permute-done | bytes 196640 | tf_op jit(solution)/shard_map/ppermute | solution.py:436
  113.8 1.7 %finish.1 = f32[384,256]{1,0:T(8,128)} custom-call(s32[4]{0:T(128)S(1)} %copy-done.2, f32[384,256]{1,0:T(8,128)S(1)} %get-tuple-element.63.total, f32[256,384]{1,0:T(8,128)S(1)} %get-tuple-element.70.here, bf16[256,384]{1,0:T(8,128)(2,1)S(1)} %collective-permute-done.5.from_lower, bf16[256,384]{1,0:T(8,128)(2,1)S(1)} %collective-permute-done.6.from_upper), custom_call_target="tpu_custom_call" | custom-call | tf_op jit(solution)/shard_map/finish/pallas_call | solution.py:619
  (16 shorter events, 0.0 us)
Async XLA Ops:
  3.2 36.4 %all-to-all-start.1 = ((bf16[16,384,128]{2,1,0:T(8,128)(2,1)}), bf16[16,384,128]{2,1,0:T(8,128)(2,1)S(1)}, u32[]{:S(2)}, u32[]{:S(2)}) async-start(bf16[16,384,128]{2,1,0:T(8,128)(2,1)} %get-tuple-element.51), calls=%async_computation.1 | async-start | bytes 3145728 | tf_op jit(solution)/shard_map/all_to_all | solution.py:488
  16.5 23.1 %collective-permute-start.1 = (s32[128,128]{1,0:T(8,128)}, s32[128,128]{1,0:T(8,128)S(1)}, u32[]{:S(2)}, u32[]{:S(2)}) collective-permute-start(s32[128,128]{1,0:T(8,128)} %get-tuple-element.52), channel_id=1, source_target_pairs={{32,0},{64,32},{96,64},{0,96},{33,1},{65,33},{97,65},{1,97},{34,2}... | collective-permute-start | bytes 196616 | tf_op jit(solution)/shard_map/ppermute | solution.py:436
  17.3 22.3 %collective-permute-start = (s32[128,128]{1,0:T(8,128)}, s32[128,128]{1,0:T(8,128)S(1)}, u32[]{:S(2)}, u32[]{:S(2)}) collective-permute-start(s32[128,128]{1,0:T(8,128)} %get-tuple-element.52), channel_id=1, source_target_pairs={{96,0},{0,32},{32,64},{64,96},{97,1},{1,33},{33,65},{65,97},{98,2}... | collective-permute-start | bytes 196616 | tf_op jit(solution)/shard_map/ppermute | solution.py:436
  39.6 59.7 %all-to-all-start.2 = ((bf16[32,496,128]{2,1,0:T(8,128)(2,1)}), bf16[32,496,128]{2,1,0:T(8,128)(2,1)}, u32[]{:S(2)}, u32[]{:S(2)}) async-start(bf16[32,496,128]{2,1,0:T(8,128)(2,1)} %get-tuple-element.53), calls=%async_computation.2 | async-start | bytes 8126464 | tf_op jit(solution)/shard_map/all_to_all | solution.py:522
  47.2 6.9 %copy-start = (bf16[192,256]{1,0:T(8,128)(2,1)S(1)}, bf16[192,256]{1,0:T(8,128)(2,1)}, u32[]{:S(2)}) copy-start(bf16[192,256]{1,0:T(8,128)(2,1)} %get-tuple-element.48.guess) | copy-start | bytes 294916
  47.3 6.9 %copy-start.1 = (bf16[1152,256]{1,0:T(8,128)(2,1)S(1)}, bf16[1152,256]{1,0:T(8,128)(2,1)}, u32[]{:S(2)}) copy-start(bf16[1152,256]{1,0:T(8,128)(2,1)} %blocks.4) | copy-start | bytes 1769476
  47.3 25.8 %copy-start.2 = (s32[4]{0:T(128)S(1)}, s32[4]{0:T(128)}, u32[]{:S(2)}) copy-start(s32[4]{0:T(128)} %pad_add_fusion.info) | copy-start | bytes 52
  47.3 25.8 %copy-start.3 = (s32[24,128]{1,0:T(8,128)S(1)}, s32[24,128]{1,0:T(8,128)}, u32[]{:S(2)}) copy-start(s32[24,128]{1,0:T(8,128)} %get-tuple-element.54) | copy-start | bytes 36868
  47.3 25.8 %copy-start.4 = (s32[24,128]{1,0:T(8,128)S(1)}, s32[24,128]{1,0:T(8,128)}, u32[]{:S(2)}) copy-start(s32[24,128]{1,0:T(8,128)} %get-tuple-element.55) | copy-start | bytes 36868
  47.3 25.8 %copy-start.5 = (s32[24,128]{1,0:T(8,128)S(1)}, s32[24,128]{1,0:T(8,128)}, u32[]{:S(2)}) copy-start(s32[24,128]{1,0:T(8,128)} %get-tuple-element.56.half) | copy-start | bytes 36868
  47.3 3.5 %collective-permute-start.2 = (bf16[16,384,128]{2,1,0:T(8,128)(2,1)S(1)}, bf16[16,384,128]{2,1,0:T(8,128)(2,1)S(1)}, u32[]{:S(2)}, u32[]{:S(2)}) collective-permute-start(bf16[16,384,128]{2,1,0:T(8,128)(2,1)S(1)} %all-to-all-done.1.same), channel_id=1, source_target_pairs={{1,0},{0,1},{3,2},{2,3},{5,4},{4,5},{7,6},{6,7},{9,8},{8,9},{11,10... | collective-permute-start | bytes 4718600 | tf_op jit(solution)/shard_map/ppermute | solution.py:524
  52.1 19.7 %collective-permute-start.3 = (bf16[32,96,128]{2,1,0:T(8,128)(2,1)S(1)}, bf16[32,96,128]{2,1,0:T(8,128)(2,1)S(1)}, u32[]{:S(2)}, u32[]{:S(2)}) collective-permute-start(bf16[32,96,128]{2,1,0:T(8,128)(2,1)S(1)} %get-tuple-element.60), channel_id=1, source_target_pairs={{96,0},{0,32},{32,64},{64,96},{97,1},{1,33},{33,65},{65,97},{98,2}... | collective-permute-start | bytes 2359304 | tf_op jit(solution)/shard_map/ppermute | solution.py:436
  52.1 20.9 %collective-permute-start.4 = (bf16[32,96,128]{2,1,0:T(8,128)(2,1)S(1)}, bf16[32,96,128]{2,1,0:T(8,128)(2,1)S(1)}, u32[]{:S(2)}, u32[]{:S(2)}) collective-permute-start(bf16[32,96,128]{2,1,0:T(8,128)(2,1)S(1)} %get-tuple-element.61), channel_id=1, source_target_pairs={{32,0},{64,32},{96,64},{0,96},{33,1},{65,33},{97,65},{1,97},{34,2}... | collective-permute-start | bytes 2359304 | tf_op jit(solution)/shard_map/ppermute | solution.py:436
  106.8 5.7 %collective-permute-start.5 = (bf16[256,384]{1,0:T(8,128)(2,1)S(1)}, bf16[256,384]{1,0:T(8,128)(2,1)S(1)}, u32[]{:S(2)}, u32[]{:S(2)}) collective-permute-start(bf16[256,384]{1,0:T(8,128)(2,1)S(1)} %get-tuple-element.71), channel_id=1, source_target_pairs={{96,0},{0,32},{32,64},{64,96},{97,1},{1,33},{33,65},{65,97},{98,2}... | collective-permute-start | bytes 589832 | tf_op jit(solution)/shard_map/ppermute | solution.py:436
  106.9 6.9 %collective-permute-start.6 = (bf16[256,384]{1,0:T(8,128)(2,1)S(1)}, bf16[256,384]{1,0:T(8,128)(2,1)S(1)}, u32[]{:S(2)}, u32[]{:S(2)}) collective-permute-start(bf16[256,384]{1,0:T(8,128)(2,1)S(1)} %get-tuple-element.72), channel_id=1, source_target_pairs={{32,0},{64,32},{96,64},{0,96},{33,1},{65,33},{97,65},{1,97},{34,2}... | collective-permute-start | bytes 589832 | tf_op jit(solution)/shard_map/ppermute | solution.py:436
